TPU v7x, 128 devices: a whole 4x4x4 slice. The times are simulated.
128 devices in a mesh: dp: 8 (over z, core), shard: 16 (over y, x).
Axes of the slice: x: 4, y: 4, z: 4, core: 2. Of those that a mesh axis runs over, the one named last changes fastest.
Arguments:
- grad_parts: float32 [8, 2048, 8192], P('dp', 'shard'), may hold values from -0.3125 to 0.3125
- moment: float32 [16, 128, 8192], P('shard', 'dp'), may hold values from -0.75 to 0.75
- second: float32 [16, 128, 8192], P('shard', 'dp'), may hold values from 0.001 to 0.01
- left_prev: float32 [8, 16, 1, 512, 512], P('dp', 'shard'), may hold values from -1 to 5, as said below
- right_prev: float32 [8, 16, 1, 512, 512], P('dp', 'shard'), may hold values from -1 to 5, as said below
- owners: int32 [64], replicated, may hold values from 0 to 15, as said below
- newton_steps: int32 [64], replicated, may hold values from 2 to 3
Outputs:
- update: float32 [16, 128, 8192], P('shard', 'dp')
- new_moment: float32 [16, 128, 8192], P('shard', 'dp')
- new_second: float32 [16, 128, 8192], P('shard', 'dp')
- new_left: float32 [8, 16, 1, 512, 512], P('dp', 'shard')
- new_right: float32 [8, 16, 1, 512, 512], P('dp', 'shard')
- root_left: float32 [8, 16, 1, 512, 512], P('dp', 'shard')
- root_right: float32 [8, 16, 1, 512, 512], P('dp', 'shard')
Inputs may be any that keep to these rules, and one draw needn't show every extreme that they name: `owners`: among the 16 blocks of any block-row at most 2 share an owner, and one shard index owns exactly 2 blocks in every block-row. `left_prev`: each slot is a symmetric positive definite matrix. `right_prev`: each slot is a symmetric positive definite matrix.
All inputs are finite; a program needn't handle non-finite values.
Results may differ from a plain program's by a relative error of at most 0.00018.
Values sent between devices are 32-bit elements; how exact they have to be, the bound alone decides.
A program may use at most 64 MiB of HBM per device.

v0:
```python
import functools

import jax
import jax.numpy as jnp
from jax import lax
from jax.experimental import pallas as pl
from jax.experimental.pallas import tpu as pltpu
from jax.sharding import PartitionSpec as P

MESH = pl.DeviceIdType.MESH
CORES = 2
SUB = 8
CAP = 2
MIB = 1 << 20


def routes(owners, newton_steps, my_dp, my_shard, dims):
    ndp, nshard, nx, nbr, nbc = dims
    ids = jnp.arange(nbr * nbc, dtype=jnp.int32)
    row = ids // nbc
    earlier = (owners[:, None] == owners[None, :]) & (ids[None, :] < ids[:, None])
    rank = jnp.sum(earlier, axis=1, dtype=jnp.int32)
    sub = jnp.sum(earlier & (row[None, :] == row[:, None]), axis=1, dtype=jnp.int32)
    my_row = my_shard // nx

    def pick(count, key, chosen, value):
        hit = (jnp.arange(count, dtype=jnp.int32)[:, None] == key[None, :]) & chosen[None, :]
        return jnp.sum(jnp.where(hit, value[None, :], 0), axis=1, dtype=jnp.int32)

    mine = owners == my_shard
    here = row == my_row
    slot = owners * CAP + sub
    column = ids % nbc
    always = jnp.full_like(ids, 1)
    sends = pick(nshard * CAP, slot, here, column)
    by_rank = pick(ndp, rank, mine, row * CAP + sub)
    by_row = pick(nbr * CAP, row * CAP + sub, mine, rank)
    finals = pick(nbc, column, here, slot)
    place = mine & (rank == my_dp)
    steps = jnp.sum(jnp.where(place, newton_steps, 0), keepdims=True)
    taken = jnp.sum(jnp.where(place, always, 0), keepdims=True)
    return jnp.concatenate([sends, by_rank, by_row, finals, steps, taken]).astype(jnp.int32)


def offsets(dims):
    ndp, nshard, nx, nbr, nbc = dims
    sends = 0
    by_rank = sends + nshard * CAP
    by_row = by_rank + ndp
    finals = by_row + nbr * CAP
    steps = finals + nbc
    return sends, by_rank, by_row, finals, steps


def greet(peers):
    barrier = pltpu.get_barrier_semaphore()
    for peer in peers:
        pl.semaphore_signal(barrier, inc=1, device_id=peer, device_id_type=MESH)
    pl.semaphore_wait(barrier, len(peers))


def forward_kernel(dims, block, chunks, tab, grad, mom, sec,
                   gblk, mom_out, sec_out, adam_out,
                   loc, pair, first_up, first_down, from_below, from_above,
                   gsel, mbuf, vbuf, send1, recv1, send2, asend, arecv, xsend, xrecv,
                   loc_sem, pair_s, pair_r, ring_s, ring_r, p1_s, p1_r, p2_s, p2_r,
                   a_s, a_r, x_s, x_r, io_sem):
    ndp, nshard, nx, nbr, nbc = dims
    o_sends, o_rank, _, _, _ = offsets(dims)
    nz = ndp // CORES
    columns = nbc * block
    half = columns // 2
    rows_dev = SUB * chunks
    me_d = lax.axis_index("dp")
    me_s = lax.axis_index("shard")
    z = me_d // CORES
    core = me_d % CORES
    my_x = me_s % nx
    my_row = me_s // nx

    def zed(step):
        return (z + step) % nz

    def rows_of(zz, cc, h):
        return pl.ds(pl.multiple_of((zz * CORES + cc) * rows_dev + h * SUB, SUB), SUB)

    order = (2, 1, nz - 1, 0)
    loads = {}
    for h in range(chunks):
        for q, step in enumerate(order):
            loads[h, q] = pltpu.make_async_copy(
                grad.at[rows_of(zed(step), core, h), :], loc.at[h, q], loc_sem.at[h, q])
            loads[h, q].start()
    m_in = pltpu.make_async_copy(mom, mbuf, io_sem.at[0])
    v_in = pltpu.make_async_copy(sec, vbuf, io_sem.at[1])
    m_in.start()
    v_in.start()

    dps = [((me_d + k) % ndp, me_s) for k in range(1, ndp)]
    shards = [(me_d, (me_s + k) % nshard) for k in range(1, nshard)]
    greet(dps + shards)

    sibling = (z * CORES + (1 - core), me_s)
    above = (zed(1) * CORES + core, me_s)
    below = (zed(nz - 1) * CORES + core, me_s)
    pairs = {}
    for h in range(chunks):
        for q, step in enumerate(order):
            pairs[h, q] = pltpu.make_async_remote_copy(
                grad.at[rows_of(zed(step), 1 - core, h), :], pair.at[h, q],
                pair_s.at[h, q], pair_r.at[h, q], device_id=sibling, device_id_type=MESH)
            pairs[h, q].start()

    lo = pl.ds(0, half)
    hi = pl.ds(half, half)
    ring = {}

    def ring_send(h, index, src, dst, target):
        copy = pltpu.make_async_remote_copy(
            src, dst, ring_s.at[h, index], ring_r.at[h, index], device_id=target, device_id_type=MESH)
        copy.start()
        ring[h, index] = copy

    def merge(h, q):
        loads[h, q].wait()
        pairs[h, q].wait_recv()
        loc[h, q] = loc[h, q] + pair[h, q]

    def ring_one(h):
        merge(h, 0)
        ring_send(h, 0, loc.at[h, 0, :, lo], first_up.at[h], above)
        ring_send(h, 1, loc.at[h, 0, :, hi], first_down.at[h], below)
        merge(h, 1)
        ring_send(h, 2, loc.at[h, 1, :, hi], from_below.at[h, :, hi], above)
        merge(h, 2)
        ring_send(h, 3, loc.at[h, 2, :, lo], from_above.at[h, :, lo], below)
        merge(h, 3)

    def ring_two(h):
        ring[h, 0].wait_recv()
        loc[h, 1, :, lo] = loc[h, 1, :, lo] + first_up[h]
        ring_send(h, 4, loc.at[h, 1, :, lo], from_below.at[h, :, lo], above)
        ring[h, 1].wait_recv()
        loc[h, 2, :, hi] = loc[h, 2, :, hi] + first_down[h]
        ring_send(h, 5, loc.at[h, 2, :, hi], from_above.at[h, :, hi], below)

    def ring_end(h):
        for index in range(2, 6):
            ring[h, index].wait_recv()
        for c in range(nbc):
            cols = pl.ds(c * block, block)
            gsel[h, c] = (loc[h, 3, :, cols] + from_below[h, :, cols]) + from_above[h, :, cols]

    p1 = {}

    def exchange_shards(h):
        for k in range(1, nshard):
            target = (me_s + k) % nshard
            for j in range(CAP):
                send1[h, k, j] = gsel[h, tab[o_sends + target * CAP + j]]
            copy = pltpu.make_async_remote_copy(
                send1.at[h, k], recv1[h].at[me_s], p1_s.at[h, k], p1_r.at[h, k],
                device_id=(me_d, target), device_id_type=MESH)
            copy.start()
            p1[h, k] = copy
        for j in range(CAP):
            recv1[h][me_s, j] = gsel[h, tab[o_sends + me_s * CAP + j]]

    p2 = {}

    def exchange_dp(h):
        for k in range(1, nshard):
            p1[h, k].wait_recv()
        for k in list(range(1, ndp)) + [0]:
            target = (me_d + k) % ndp
            place = tab[o_rank + target]
            r = place // CAP
            j = place % CAP
            for x in range(nx):
                send2[h, k, x] = recv1[h][r * nx + x, j]
            if k:
                copy = pltpu.make_async_remote_copy(
                    send2.at[h, k], gblk.at[:, me_d, h], p2_s.at[h, k], p2_r.at[h, k],
                    device_id=(target, me_s), device_id_type=MESH)
            else:
                copy = pltpu.make_async_copy(send2.at[h, 0], gblk.at[:, me_d, h], p2_s.at[h, 0])
            copy.start()
            p2[h, k] = copy

    def adam_rows(h):
        rows = pl.ds(h * SUB, SUB)
        for c in range(nbc):
            cols = pl.ds(c * block, block)
            g = gsel[h, c]
            m = 0.9 * mbuf[rows, cols] + 0.1 * g
            v = 0.99 * vbuf[rows, cols] + 0.01 * g * g
            mbuf[rows, cols] = m
            vbuf[rows, cols] = v
            a = m / (jnp.sqrt(v) + 1e-08)
            sq = jnp.sum(a * a, axis=0, keepdims=True)
            part = sq[:, 0:128]
            for t in range(1, block // 128):
                part = part + sq[:, t * 128:(t + 1) * 128]
            if h == 0:
                asend[pl.ds(c, 1), :] = part
            else:
                asend[pl.ds(c, 1), :] = asend[pl.ds(c, 1), :] + part

    ring_one(0)
    ring_two(0)
    for h in range(1, chunks):
        ring_one(h)
    m_in.wait()
    v_in.wait()
    ring_end(0)
    exchange_shards(0)
    adam_rows(0)
    for h in range(1, chunks):
        ring_two(h)
        ring_end(h)
        exchange_shards(h)
        exchange_dp(h - 1)
        adam_rows(h)

    m_out = pltpu.make_async_copy(mbuf, mom_out, io_sem.at[0])
    v_out = pltpu.make_async_copy(vbuf, sec_out, io_sem.at[1])
    m_out.start()
    v_out.start()
    acopies = []
    for k in range(1, ndp):
        copy = pltpu.make_async_remote_copy(
            asend, arecv.at[k], a_s.at[k], a_r.at[k],
            device_id=((me_d + k) % ndp, me_s), device_id_type=MESH)
        copy.start()
        acopies.append(copy)
    exchange_dp(chunks - 1)
    total = asend[...]
    for k in range(1, ndp):
        acopies[k - 1].wait_recv()
        total = total + arecv[k]
    xsend[...] = total
    xcopies = []
    for k in range(1, nx):
        copy = pltpu.make_async_remote_copy(
            xsend, xrecv.at[k], x_s.at[k], x_r.at[k],
            device_id=(me_d, my_row * nx + (my_x + k) % nx), device_id_type=MESH)
        copy.start()
        xcopies.append(copy)
    for k in range(1, nx):
        xcopies[k - 1].wait_recv()
        total = total + xrecv[k]
    summed = jnp.sum(total, axis=1, keepdims=True)
    arecv[0] = jnp.broadcast_to(jnp.sqrt(summed), arecv.shape[1:])
    a_out = pltpu.make_async_copy(arecv.at[0], adam_out, io_sem.at[2])
    a_out.start()

    for h in range(chunks):
        for q in range(len(order)):
            pairs[h, q].wait_send()
        for index in range(6):
            ring[h, index].wait_send()
        for k in range(1, nshard):
            p1[h, k].wait_send()
        for k in range(1, ndp):
            p2[h, k].wait_send()
            p2[h, k].wait_recv()
        p2[h, 0].wait()
    for copy in acopies + xcopies:
        copy.wait_send()
    m_out.wait()
    v_out.wait()
    a_out.wait()


def forward(tab, grad, mom, sec, dims, block):
    ndp, nshard, nx, nbr, nbc = dims
    rows_dev, columns = mom.shape
    chunks = rows_dev // SUB
    half = columns // 2
    f32 = jnp.float32
    anywhere = pl.BlockSpec(memory_space=pl.ANY)
    dma = pltpu.SemaphoreType.DMA
    body = functools.partial(forward_kernel, dims, block, chunks)
    return pl.pallas_call(
        body,
        out_shape=(
            jax.ShapeDtypeStruct((nx, ndp, chunks, SUB, block), f32),
            jax.ShapeDtypeStruct((rows_dev, columns), f32),
            jax.ShapeDtypeStruct((rows_dev, columns), f32),
            jax.ShapeDtypeStruct((nbc, 128), f32),
        ),
        in_specs=[pl.BlockSpec(memory_space=pltpu.SMEM), anywhere, anywhere, anywhere],
        out_specs=(anywhere,) * 4,
        scratch_shapes=[
            pltpu.VMEM((chunks, 4, SUB, columns), f32),
            pltpu.VMEM((chunks, 4, SUB, columns), f32),
            pltpu.VMEM((chunks, SUB, half), f32),
            pltpu.VMEM((chunks, SUB, half), f32),
            pltpu.VMEM((chunks, SUB, columns), f32),
            pltpu.VMEM((chunks, SUB, columns), f32),
            pltpu.VMEM((chunks, nbc, SUB, block), f32),
            pltpu.VMEM((rows_dev, columns), f32),
            pltpu.VMEM((rows_dev, columns), f32),
            pltpu.VMEM((chunks, nshard, CAP, SUB, block), f32),
            [pltpu.VMEM((nshard, CAP, SUB, block), f32) for _ in range(chunks)],
            pltpu.VMEM((chunks, ndp, nx, SUB, block), f32),
            pltpu.VMEM((nbc, 128), f32),
            pltpu.VMEM((ndp, nbc, 128), f32),
            pltpu.VMEM((nbc, 128), f32),
            pltpu.VMEM((nx, nbc, 128), f32),
            dma((chunks, 4)),
            dma((chunks, 4)),
            dma((chunks, 4)),
            dma((chunks, 6)),
            dma((chunks, 6)),
            dma((chunks, nshard)),
            dma((chunks, nshard)),
            dma((chunks, ndp)),
            dma((chunks, ndp)),
            dma((ndp,)),
            dma((ndp,)),
            dma((nx,)),
            dma((nx,)),
            dma((3,)),
        ],
        compiler_params=pltpu.CompilerParams(
            collective_id=0, has_side_effects=True, vmem_limit_bytes=40 * MIB),
    )(tab, grad, mom, sec)


def split(value):
    high = value.astype(jnp.bfloat16)
    low = (value - high.astype(jnp.float32)).astype(jnp.bfloat16)
    return high, low


def product(first, second_factor, axes=((1,), (0,))):
    def dot(left, right):
        return lax.dot_general(left, right, (axes, ((), ())), preferred_element_type=jnp.float32)

    return dot(first[0], second_factor[0]) + (
        dot(first[0], second_factor[1]) + dot(first[1], second_factor[0]))


def owner_kernel(step_place, tab, gblk, left_prev, right_prev, mom, sec,
                 left_out, right_out, lroot_out, rroot_out, dir_out, mom_out, sec_out,
                 g_ref, stat, root, cur, sem):
    taken = tab[step_place + 1]
    m_copy = pltpu.make_async_copy(mom, mom_out, sem.at[0])
    v_copy = pltpu.make_async_copy(sec, sec_out, sem.at[1])
    m_copy.start()
    v_copy.start()
    size = g_ref.shape[0]
    outs = (left_out, right_out, lroot_out, rroot_out, dir_out)

    @pl.when(taken == 0)
    def _():
        stat[0] = jnp.zeros_like(stat[0])
        copies = [pltpu.make_async_copy(stat.at[0], out, sem.at[2 + i]) for i, out in enumerate(outs)]
        for copy in copies:
            copy.start()
        for copy in copies:
            copy.wait()

    @pl.when(taken != 0)
    def _():
        g_in = pltpu.make_async_copy(gblk, g_ref, sem.at[2])
        ins = [pltpu.make_async_copy(prev, stat.at[i], sem.at[3 + i])
               for i, prev in enumerate((left_prev, right_prev))]
        g_in.start()
        for copy in ins:
            copy.start()
        r_ids = lax.broadcasted_iota(jnp.int32, (size, size), 0)
        c_ids = lax.broadcasted_iota(jnp.int32, (size, size), 1)
        diagonal = r_ids == c_ids

        def complement(matrix):
            return jnp.where(diagonal, 1.25, 0.0) - 0.25 * matrix

        g_in.wait()
        g = split(g_ref[...])
        scales = []
        stat_outs = []
        for i, axes in enumerate((((1,), (1,)), ((0,), (0,)))):
            gram = product(g, g, axes)
            ins[i].wait()
            stat[i] = 0.95 * stat[i] + gram
            copy = pltpu.make_async_copy(stat.at[i], outs[i], sem.at[3 + i])
            copy.start()
            stat_outs.append(copy)
        for i in range(2):
            shifted = stat[i] + jnp.where(diagonal, 0.0001, 0.0)
            norm = jnp.sum(shifted * shifted)
            scale = 2.5 / jnp.sqrt(jnp.full((1, 1), norm))
            cur[i] = scale * shifted
            scales.append(jnp.sqrt(jnp.sqrt(scale)))

        def raise_four(factor, matrix):
            square = split(product(factor, factor))
            return product(square, split(product(square, matrix)))

        for i in range(2):
            matrix = cur[i]
            factor = split(complement(matrix))
            after = raise_four(factor, split(matrix))
            cur[i] = after
            root[i] = scales[i] * product(factor, split(complement(after)))

        @pl.when(tab[step_place] > 2)
        def _():
            for i in range(2):
                matrix = cur[i]
                after = raise_four(split(complement(matrix)), split(matrix))
                root[i] = product(split(root[i]), split(complement(after)))

        root_outs = []
        for i in range(2):
            copy = pltpu.make_async_copy(root.at[i], outs[2 + i], sem.at[5 + i])
            copy.start()
            root_outs.append(copy)
        for copy in stat_outs:
            copy.wait()
        way = product(split(product(split(root[0]), g)), split(root[1]))
        power = jnp.sum(way * way)
        g_ref[...] = way / jnp.sqrt(jnp.full((1, 1), power) + 1e-12)
        d_out = pltpu.make_async_copy(g_ref, dir_out, sem.at[2])
        d_out.start()
        for copy in root_outs:
            copy.wait()
        d_out.wait()

    m_copy.wait()
    v_copy.wait()


def owner_step(tab, gblk, left_prev, right_prev, mom, sec, step_place):
    size = gblk.shape[0]
    f32 = jnp.float32
    square = jax.ShapeDtypeStruct((size, size), f32)
    anywhere = pl.BlockSpec(memory_space=pl.ANY)
    return pl.pallas_call(
        functools.partial(owner_kernel, step_place),
        out_shape=(square,) * 5 + (jax.ShapeDtypeStruct(mom.shape, f32),) * 2,
        in_specs=[pl.BlockSpec(memory_space=pltpu.SMEM)] + [anywhere] * 5,
        out_specs=(anywhere,) * 7,
        scratch_shapes=[
            pltpu.VMEM((size, size), f32),
            pltpu.VMEM((2, size, size), f32),
            pltpu.VMEM((2, size, size), f32),
            pltpu.VMEM((2, size, size), f32),
            pltpu.SemaphoreType.DMA((7,)),
        ],
        compiler_params=pltpu.CompilerParams(vmem_limit_bytes=56 * MIB),
        cost_estimate=pl.CostEstimate(
            flops=120 * size ** 3, bytes_accessed=36 * size * size, transcendentals=0),
    )(tab, gblk, left_prev, right_prev, mom, sec)


def back_kernel(dims, block, chunks, tab, way, adam, update,
                recv2, send1, recv1, out, ad, p2_s, p2_r, p1_s, p1_r, io_sem):
    ndp, nshard, nx, nbr, nbc = dims
    _, _, o_row, o_final, _ = offsets(dims)
    me_d = lax.axis_index("dp")
    me_s = lax.axis_index("shard")
    a_in = pltpu.make_async_copy(adam, ad, io_sem.at[0])
    a_in.start()
    dps = [((me_d + k) % ndp, me_s) for k in range(1, ndp)]
    shards = [(me_d, (me_s + k) % nshard) for k in range(1, nshard)]
    greet(dps + shards)
    p2 = {}
    for h in range(chunks):
        for k in range(1, ndp):
            target = (me_d + k) % ndp
            copy = pltpu.make_async_remote_copy(
                way.at[:, target, h], recv2[h].at[me_d], p2_s.at[h, k], p2_r.at[h, k],
                device_id=(target, me_s), device_id_type=MESH)
            copy.start()
            p2[h, k] = copy
        copy = pltpu.make_async_copy(way.at[:, me_d, h], recv2[h].at[me_d], p2_s.at[h, 0])
        copy.start()
        p2[h, 0] = copy
    p1 = {}
    for h in range(chunks):
        for k in range(1, ndp):
            p2[h, k].wait_recv()
        p2[h, 0].wait()
        for k in range(1, nshard):
            target = (me_s + k) % nshard
            r = target // nx
            x = target % nx
            for j in range(CAP):
                send1[h, k, j] = recv2[h][tab[o_row + r * CAP + j], x]
            copy = pltpu.make_async_remote_copy(
                send1.at[h, k], recv1[h].at[pl.ds(me_s * CAP, CAP)], p1_s.at[h, k], p1_r.at[h, k],
                device_id=(me_d, target), device_id_type=MESH)
            copy.start()
            p1[h, k] = copy
        for j in range(CAP):
            recv1[h][me_s * CAP + j] = recv2[h][tab[o_row + (me_s // nx) * CAP + j], me_s % nx]
    a_in.wait()
    outs = []
    for h in range(chunks):
        for k in range(1, nshard):
            p1[h, k].wait_recv()
        rows = pl.ds(h * SUB, SUB)
        for c in range(nbc):
            scale = jnp.concatenate([ad[pl.ds(c, 1), :]] * (block // 128), axis=1)
            out[rows, pl.ds(c * block, block)] = recv1[h][tab[o_final + c]] * scale
        copy = pltpu.make_async_copy(out.at[rows, :], update.at[rows, :], io_sem.at[1 + h])
        copy.start()
        outs.append(copy)
    for h in range(chunks):
        for k in range(1, ndp):
            p2[h, k].wait_send()
        for k in range(1, nshard):
            p1[h, k].wait_send()
        outs[h].wait()


def back(tab, way, adam, dims, block, rows_dev, columns):
    ndp, nshard, nx, nbr, nbc = dims
    chunks = rows_dev // SUB
    f32 = jnp.float32
    anywhere = pl.BlockSpec(memory_space=pl.ANY)
    dma = pltpu.SemaphoreType.DMA
    return pl.pallas_call(
        functools.partial(back_kernel, dims, block, chunks),
        out_shape=jax.ShapeDtypeStruct((rows_dev, columns), f32),
        in_specs=[pl.BlockSpec(memory_space=pltpu.SMEM), anywhere, anywhere],
        out_specs=anywhere,
        scratch_shapes=[
            [pltpu.VMEM((ndp, nx, SUB, block), f32) for _ in range(chunks)],
            pltpu.VMEM((chunks, nshard, CAP, SUB, block), f32),
            [pltpu.VMEM((nshard * CAP, SUB, block), f32) for _ in range(chunks)],
            pltpu.VMEM((rows_dev, columns), f32),
            pltpu.VMEM((nbc, 128), f32),
            dma((chunks, ndp)),
            dma((chunks, ndp)),
            dma((chunks, nshard)),
            dma((chunks, nshard)),
            dma((1 + chunks,)),
        ],
        compiler_params=pltpu.CompilerParams(
            collective_id=1, has_side_effects=True, vmem_limit_bytes=40 * MIB),
    )(tab, way, adam)


def local(grad_parts, moment, second, left_prev, right_prev, owners, newton_steps):
    ndp = lax.axis_size("dp")
    nshard = lax.axis_size("shard")
    my_dp = lax.axis_index("dp")
    my_shard = lax.axis_index("shard")
    _, rows_dev, columns = moment.shape
    block = left_prev.shape[-1]
    nx = block // (rows_dev * ndp)
    dims = (ndp, nshard, nx, nshard // nx, columns // block)
    tab = routes(owners, newton_steps, my_dp, my_shard, dims)
    gblk, mom, sec, adam = forward(tab, grad_parts[0], moment[0], second[0], dims, block)
    place = offsets(dims)[4]
    left, right, lroot, rroot, way, mom, sec = owner_step(
        tab, gblk.reshape(block, block), left_prev[0, 0, 0], right_prev[0, 0, 0], mom, sec, place)
    chunks = rows_dev // SUB
    update = back(tab, way.reshape(nx, ndp, chunks, SUB, block), adam, dims, block, rows_dev, columns)
    slots = (1, 1, 1, block, block)
    return (
        update[None],
        mom[None],
        sec[None],
        left.reshape(slots),
        right.reshape(slots),
        lroot.reshape(slots),
        rroot.reshape(slots),
    )


def solution(mesh):
    rows = P("shard", "dp", None)
    slots = P("dp", "shard", None, None, None)
    return jax.shard_map(
        local,
        mesh=mesh,
        in_specs=(P("dp", "shard", None), rows, rows, slots, slots, P(), P()),
        out_specs=(rows, rows, rows, slots, slots, slots, slots),
        check_vma=False,
    )
```

profile of v0, /device:TPU:1, one launch (start us, length us, event | category | flops | bytes accessed | tf_op | source)
XLA Modules:
  0.0 123.1 jit_solution(2348871925670334258)
XLA Ops:
  0.7 0.9 convert_reduce_fusion
  1.6 1.3 %select_reduce_fusion.4 = (s32[]{:T(128)}, s32[]{:T(128)}, pred[64]{0:T(512)(128)(4,1)S(1)}, s32[64]{0:T(128)S(1)}, s32[64]{0:T(128)S(1)}, /*index=5*/s32[64]{0:T(128)S(1)}) fusion(s32[64]{0:T(128)S(1)} %get-tuple-element.33, s32[]{:T(128)S(6)} %axis_index.25, s32[64]{0:T(128)} %param.13, s32[64]{0:T(128)} %param.12, s32[]{:T(128)S(6)} %axis_index.22, ...), kind=kLoop, calls=%fused_computation.22 | loop fusion | flops 1470 | bytes 1872 | tf_op jit(solution)/shard_map/reduce_sum | solution.py:41
  2.9 0.1 select_reduce_fusion.2
  3.1 0.1 select_reduce_fusion.1
  3.2 0.1 select_reduce_fusion
  3.3 1.4 %concatenate.3.tab = s32[66]{0:T(128)S(1)} concatenate(s32[32]{0:T(128)S(1)} %select_reduce_fusion, s32[8]{0:T(128)S(1)} %get-tuple-element.30, s32[8]{0:T(128)S(1)} %get-tuple-element.29, s32[16]{0:T(128)S(1)} %select_reduce_fusion.1, s32[1]{0:T(128)} %bitcast, s32[1]{0:T(128)} %bitcast.1), dimensions={0} | concatenate | bytes 528 | tf_op jit(solution)/shard_map/concatenate | solution.py:42
  4.7 0.0 copy-start
  4.7 2.2 %copy-done = f32[1,128,8192]{2,1,0:T(8,128)S(1)} copy-done((f32[1,128,8192]{2,1,0:T(8,128)S(1)}, f32[1,128,8192]{2,1,0:T(8,128)}, u32[]{:S(2)}) %copy-start) | copy-done | bytes 4194328
  6.9 0.0 copy-start.2
  6.9 1.0 copy-done.2
  7.9 0.0 copy-start.3
  7.9 1.0 copy-done.3
  9.0 0.0 copy-start.4
  9.0 47.8 %shard_map.126 = (f32[4,8,2,8,512]{4,3,2,1,0:T(8,128)S(1)}, f32[16,8192]{1,0:T(8,128)S(1)}, f32[16,8192]{1,0:T(8,128)S(1)}, f32[16,128]{1,0:T(8,128)S(1)}) custom-call(s32[66]{0:T(128)S(1)} %concatenate.3.tab, f32[128,8192]{1,0:T(8,128)S(1)} %bitcast.16, f32[16,8192]{1,0:T(8,128)S(1)} %bitcast.19, f32[16,8192]{1,0:T(8,128)S(1)} %bitcast.20), custom_call_target="tpu_custom_call" | custom-call | tf_op jit(solution)/shard_map/pallas_call | solution.py:284
  56.8 0.0 copy-start.6
  56.8 1.0 copy-done.6
  57.8 0.0 copy-start.7
  57.8 0.8 copy-done.7
  58.6 0.0 copy-start.8
  58.6 0.8 copy-done.8
  59.4 0.0 copy-done.4
  59.4 33.6 %shard_map.127 = (f32[512,512]{1,0:T(8,128)}, f32[512,512]{1,0:T(8,128)}, f32[512,512]{1,0:T(8,128)}, f32[512,512]{1,0:T(8,128)}, f32[512,512]{1,0:T(8,128)}, /*index=5*/f32[16,8192]{1,0:T(8,128)}, f32[16,8192]{1,0:T(8,128)}) custom-call(s32[66]{0:T(128)} %copy-done.4, f32[512,512]{1,0:T(8,128)} %bitcast.21, f32[512,512]{1,0:T(8,128)} %bitcast.22, ...), custom_call_target="tpu_custom_call" | custom-call | flops 16106127360 | bytes 9437184 | tf_op jit(solution)/shard_map/pallas_call | solution.py:441
  93.0 0.0 copy-start.1
  93.0 1.2 copy-done.1
  94.2 0.0 copy-start.5
  94.2 0.6 copy-done.5
  94.8 27.5 %shard_map.128 = f32[16,8192]{1,0:T(8,128)S(1)} custom-call(s32[66]{0:T(128)S(1)} %copy-done.5, f32[4,8,2,8,512]{4,3,2,1,0:T(8,128)S(1)} %bitcast.18, f32[16,128]{1,0:T(8,128)S(1)} %get-tuple-element.22.adam), custom_call_target="tpu_custom_call" | custom-call | tf_op jit(solution)/shard_map/pallas_call | solution.py:526
  122.3 0.8 copy.15
  (2 shorter events, 0.0 us)
Async XLA Ops:
  4.7 2.2 %copy-start = (f32[1,128,8192]{2,1,0:T(8,128)S(1)}, f32[1,128,8192]{2,1,0:T(8,128)}, u32[]{:S(2)}) copy-start(f32[1,128,8192]{2,1,0:T(8,128)} %param.7) | copy-start | bytes 12582916
  6.9 1.0 copy-start.2
  7.9 1.0 copy-start.3
  9.0 50.4 %copy-start.4 = (s32[66]{0:T(128)}, s32[66]{0:T(128)S(1)}, u32[]{:S(2)}) copy-start(s32[66]{0:T(128)S(1)} %concatenate.3.tab) | copy-start | bytes 796
  56.8 1.0 copy-start.6
  57.8 0.8 copy-start.7
  58.6 0.8 copy-start.8
  93.0 1.2 copy-start.1
  94.2 0.6 copy-start.5
where the time goes:
time: 123 us
  Pallas kernels  109 us (89%)
  local copies, waits for them, and re-layouts  10.8 us (9%)
  other arithmetic  2.63 us (2%)
    pallas_call x1, Pallas kernels, forward(): pl.pallas_call(body, out_shape=(jax.ShapeDtypeStruct((nx, ndp, chunks, SU...  47.8 us
    pallas_call x1, Pallas kernels, owner_step(): pl.pallas_call(functools.partial(owner_kernel, step_place), out_shape=(sq...  33.6 us
    pallas_call x1, Pallas kernels, back(): pl.pallas_call(functools.partial(back_kernel, dims, block, chunks), out_s...  27.5 us
    unnamed x19, local copies, waits for them, and re-layouts  9.47 us

commit v1 on v0

v1 whole, which is shorter than its diff:
```python
import functools

import jax
import jax.numpy as jnp
from jax import lax
from jax.experimental import pallas as pl
from jax.experimental.pallas import tpu as pltpu
from jax.sharding import PartitionSpec as P

MESH = pl.DeviceIdType.MESH
CORES = 2
SUB = 8
CAP = 2
MIB = 1 << 20


def route_table(own, steps, my_dp, my_shard, dims):
    ndp, nshard, nx, nbr, nbc = dims
    count = nbr * nbc
    o_sends, o_rank, o_row, o_final, o_steps = offsets(dims)
    down = lax.broadcasted_iota(jnp.int32, (count, count), 0)
    across = lax.broadcasted_iota(jnp.int32, (count, count), 1)
    wide = jnp.broadcast_to(own, (count, count))

    def turned(row):
        return jnp.sum(jnp.where(down == across, jnp.broadcast_to(row, (count, count)), 0), axis=1, keepdims=True)

    owner = turned(own)
    earlier = jnp.where((owner == wide) & (across < down), 1, 0)
    rank = jnp.sum(earlier, axis=1, keepdims=True)
    sub = jnp.sum(jnp.where(across // nbc == down // nbc, earlier, 0), axis=1, keepdims=True)
    count_of = turned(steps)
    lane = lax.broadcasted_iota(jnp.int32, (count, 128), 1)
    block = lax.broadcasted_iota(jnp.int32, (count, 128), 0)

    def spread(column):
        return jnp.broadcast_to(column, (count, 128))

    owner, rank, sub, count_of = (spread(column) for column in (owner, rank, sub, count_of))
    row, column = block // nbc, block % nbc
    mine = jnp.where(owner == my_shard, 1, 0)
    here = jnp.where(row == my_shard // nx, 1, 0)
    slot = owner * CAP + sub
    place = row * CAP + sub
    key = jnp.where(lane < o_rank, slot, jnp.where(lane < o_row, rank + o_rank, jnp.where(
        lane < o_final, place + o_row, jnp.where(lane < o_steps, column + o_final, -1))))
    value = jnp.where(lane < o_rank, column, jnp.where(lane < o_row, place, jnp.where(
        lane < o_final, rank, slot)))
    chosen = jnp.where((lane < o_rank) | (lane >= o_final), here, mine)
    table = jnp.where(key == lane, value * chosen, 0)
    held = jnp.where(rank == my_dp, mine, 0)
    table = table + jnp.where(lane == o_steps, held * count_of, jnp.where(lane == o_steps + 1, held, 0))
    return jnp.sum(table, axis=0, keepdims=True)


def offsets(dims):
    ndp, nshard, nx, nbr, nbc = dims
    sends = 0
    by_rank = sends + nshard * CAP
    by_row = by_rank + ndp
    finals = by_row + nbr * CAP
    steps = finals + nbc
    return sends, by_rank, by_row, finals, steps


def greet(peers):
    barrier = pltpu.get_barrier_semaphore()
    for peer in peers:
        pl.semaphore_signal(barrier, inc=1, device_id=peer, device_id_type=MESH)
    pl.semaphore_wait(barrier, len(peers))


def forward_kernel(dims, block, chunks, own, steps, grad, mom, sec,
                   gblk, mom_out, sec_out, adam_out, tab_out,
                   ibuf, tvec, tab, loc, pair, first_up, first_down, from_below, from_above,
                   gsel, mbuf, vbuf, send1, recv1, send2, asend, arecv, xsend, xrecv,
                   loc_sem, pair_s, pair_r, ring_s, ring_r, p1_s, p1_r, p2_s, p2_r,
                   a_s, a_r, x_s, x_r, io_sem, t_sem):
    ndp, nshard, nx, nbr, nbc = dims
    o_sends, o_rank, _, _, _ = offsets(dims)
    nz = ndp // CORES
    columns = nbc * block
    half = columns // 2
    rows_dev = SUB * chunks
    me_d = lax.axis_index("dp")
    me_s = lax.axis_index("shard")
    z = me_d // CORES
    core = me_d % CORES
    my_x = me_s % nx
    my_row = me_s // nx

    def zed(step):
        return (z + step) % nz

    def rows_of(zz, cc, h):
        return pl.ds(pl.multiple_of((zz * CORES + cc) * rows_dev + h * SUB, SUB), SUB)

    order = (2, 1, nz - 1, 0)
    loads = {}
    lists = [pltpu.make_async_copy(src, ibuf.at[i], t_sem.at[i]) for i, src in enumerate((own, steps))]
    for copy in lists:
        copy.start()
    for h in range(chunks):
        for q, step in enumerate(order):
            loads[h, q] = pltpu.make_async_copy(
                grad.at[rows_of(zed(step), core, h), :], loc.at[h, q], loc_sem.at[h, q])
            loads[h, q].start()
    m_in = pltpu.make_async_copy(mom, mbuf, io_sem.at[0])
    v_in = pltpu.make_async_copy(sec, vbuf, io_sem.at[1])
    m_in.start()
    v_in.start()

    dps = [((me_d + k) % ndp, me_s) for k in range(1, ndp)]
    shards = [(me_d, (me_s + k) % nshard) for k in range(1, nshard)]
    greet(dps + shards)

    sibling = (z * CORES + (1 - core), me_s)
    above = (zed(1) * CORES + core, me_s)
    below = (zed(nz - 1) * CORES + core, me_s)
    pairs = {}
    for h in range(chunks):
        for q, step in enumerate(order):
            pairs[h, q] = pltpu.make_async_remote_copy(
                grad.at[rows_of(zed(step), 1 - core, h), :], pair.at[h, q],
                pair_s.at[h, q], pair_r.at[h, q], device_id=sibling, device_id_type=MESH)
            pairs[h, q].start()

    for copy in lists:
        copy.wait()
    tvec[...] = route_table(ibuf[0], ibuf[1], me_d, me_s, dims)
    table_in = pltpu.make_async_copy(tvec, tab, t_sem.at[0])
    table_in.start()
    table_out = pltpu.make_async_copy(tvec, tab_out, t_sem.at[1])
    table_out.start()

    lo = pl.ds(0, half)
    hi = pl.ds(half, half)
    ring = {}

    def ring_send(h, index, src, dst, target):
        copy = pltpu.make_async_remote_copy(
            src, dst, ring_s.at[h, index], ring_r.at[h, index], device_id=target, device_id_type=MESH)
        copy.start()
        ring[h, index] = copy

    def merge(h, q):
        loads[h, q].wait()
        pairs[h, q].wait_recv()
        loc[h, q] = loc[h, q] + pair[h, q]

    def ring_one(h):
        merge(h, 0)
        ring_send(h, 0, loc.at[h, 0, :, lo], first_up.at[h], above)
        ring_send(h, 1, loc.at[h, 0, :, hi], first_down.at[h], below)
        merge(h, 1)
        ring_send(h, 2, loc.at[h, 1, :, hi], from_below.at[h, :, hi], above)
        merge(h, 2)
        ring_send(h, 3, loc.at[h, 2, :, lo], from_above.at[h, :, lo], below)
        merge(h, 3)

    def ring_two(h):
        ring[h, 0].wait_recv()
        loc[h, 1, :, lo] = loc[h, 1, :, lo] + first_up[h]
        ring_send(h, 4, loc.at[h, 1, :, lo], from_below.at[h, :, lo], above)
        ring[h, 1].wait_recv()
        loc[h, 2, :, hi] = loc[h, 2, :, hi] + first_down[h]
        ring_send(h, 5, loc.at[h, 2, :, hi], from_above.at[h, :, hi], below)

    def ring_end(h):
        for index in range(2, 6):
            ring[h, index].wait_recv()
        for c in range(nbc):
            cols = pl.ds(c * block, block)
            gsel[h, c] = (loc[h, 3, :, cols] + from_below[h, :, cols]) + from_above[h, :, cols]

    p1 = {}

    def exchange_shards(h):
        for k in range(1, nshard):
            target = (me_s + k) % nshard
            for j in range(CAP):
                send1[h, k, j] = gsel[h, tab[0, o_sends + target * CAP + j]]
            copy = pltpu.make_async_remote_copy(
                send1.at[h, k], recv1[h].at[me_s], p1_s.at[h, k], p1_r.at[h, k],
                device_id=(me_d, target), device_id_type=MESH)
            copy.start()
            p1[h, k] = copy
        for j in range(CAP):
            recv1[h][me_s, j] = gsel[h, tab[0, o_sends + me_s * CAP + j]]

    p2 = {}

    def exchange_dp(h):
        for k in range(1, nshard):
            p1[h, k].wait_recv()
        for k in list(range(1, ndp)) + [0]:
            target = (me_d + k) % ndp
            place = tab[0, o_rank + target]
            r = place // CAP
            j = place % CAP
            for x in range(nx):
                send2[h, k, x] = recv1[h][r * nx + x, j]
            if k:
                copy = pltpu.make_async_remote_copy(
                    send2.at[h, k], gblk.at[:, me_d, h], p2_s.at[h, k], p2_r.at[h, k],
                    device_id=(target, me_s), device_id_type=MESH)
            else:
                copy = pltpu.make_async_copy(send2.at[h, 0], gblk.at[:, me_d, h], p2_s.at[h, 0])
            copy.start()
            p2[h, k] = copy

    def adam_rows(h):
        rows = pl.ds(h * SUB, SUB)
        for c in range(nbc):
            cols = pl.ds(c * block, block)
            g = gsel[h, c]
            m = 0.9 * mbuf[rows, cols] + 0.1 * g
            v = 0.99 * vbuf[rows, cols] + 0.01 * g * g
            mbuf[rows, cols] = m
            vbuf[rows, cols] = v
            a = m / (jnp.sqrt(v) + 1e-08)
            sq = jnp.sum(a * a, axis=0, keepdims=True)
            part = sq[:, 0:128]
            for t in range(1, block // 128):
                part = part + sq[:, t * 128:(t + 1) * 128]
            if h == 0:
                asend[pl.ds(c, 1), :] = part
            else:
                asend[pl.ds(c, 1), :] = asend[pl.ds(c, 1), :] + part

    ring_one(0)
    ring_two(0)
    for h in range(1, chunks):
        ring_one(h)
    m_in.wait()
    v_in.wait()
    table_in.wait()
    ring_end(0)
    exchange_shards(0)
    adam_rows(0)
    for h in range(1, chunks):
        ring_two(h)
        ring_end(h)
        exchange_shards(h)
        exchange_dp(h - 1)
        adam_rows(h)

    m_out = pltpu.make_async_copy(mbuf, mom_out, io_sem.at[0])
    v_out = pltpu.make_async_copy(vbuf, sec_out, io_sem.at[1])
    m_out.start()
    v_out.start()
    acopies = []
    for k in range(1, ndp):
        copy = pltpu.make_async_remote_copy(
            asend, arecv.at[k], a_s.at[k], a_r.at[k],
            device_id=((me_d + k) % ndp, me_s), device_id_type=MESH)
        copy.start()
        acopies.append(copy)
    exchange_dp(chunks - 1)
    total = asend[...]
    for k in range(1, ndp):
        acopies[k - 1].wait_recv()
        total = total + arecv[k]
    xsend[...] = total
    xcopies = []
    for k in range(1, nx):
        copy = pltpu.make_async_remote_copy(
            xsend, xrecv.at[k], x_s.at[k], x_r.at[k],
            device_id=(me_d, my_row * nx + (my_x + k) % nx), device_id_type=MESH)
        copy.start()
        xcopies.append(copy)
    for k in range(1, nx):
        xcopies[k - 1].wait_recv()
        total = total + xrecv[k]
    summed = jnp.sum(total, axis=1, keepdims=True)
    arecv[0] = jnp.broadcast_to(jnp.sqrt(summed), arecv.shape[1:])
    a_out = pltpu.make_async_copy(arecv.at[0], adam_out, io_sem.at[2])
    a_out.start()

    for h in range(chunks):
        for q in range(len(order)):
            pairs[h, q].wait_send()
        for index in range(6):
            ring[h, index].wait_send()
        for k in range(1, nshard):
            p1[h, k].wait_send()
        for k in range(1, ndp):
            p2[h, k].wait_send()
            p2[h, k].wait_recv()
        p2[h, 0].wait()
    for copy in acopies + xcopies:
        copy.wait_send()
    m_out.wait()
    v_out.wait()
    a_out.wait()
    table_out.wait()


def forward(own, steps, grad, mom, sec, dims, block):
    ndp, nshard, nx, nbr, nbc = dims
    rows_dev, columns = mom.shape
    chunks = rows_dev // SUB
    half = columns // 2
    f32 = jnp.float32
    anywhere = pl.BlockSpec(memory_space=pltpu.HBM)
    dma = pltpu.SemaphoreType.DMA
    body = functools.partial(forward_kernel, dims, block, chunks)
    return pl.pallas_call(
        body,
        out_shape=(
            jax.ShapeDtypeStruct((nx, ndp, chunks, SUB, block), f32),
            jax.ShapeDtypeStruct((rows_dev, columns), f32),
            jax.ShapeDtypeStruct((rows_dev, columns), f32),
            jax.ShapeDtypeStruct((nbc, 128), f32),
            jax.ShapeDtypeStruct((1, 128), jnp.int32),
        ),
        in_specs=[anywhere] * 5,
        out_specs=(anywhere,) * 5,
        scratch_shapes=[
            pltpu.VMEM((2, 1, nbr * nbc), jnp.int32),
            pltpu.VMEM((1, 128), jnp.int32),
            pltpu.SMEM((1, 128), jnp.int32),
            pltpu.VMEM((chunks, 4, SUB, columns), f32),
            pltpu.VMEM((chunks, 4, SUB, columns), f32),
            pltpu.VMEM((chunks, SUB, half), f32),
            pltpu.VMEM((chunks, SUB, half), f32),
            pltpu.VMEM((chunks, SUB, columns), f32),
            pltpu.VMEM((chunks, SUB, columns), f32),
            pltpu.VMEM((chunks, nbc, SUB, block), f32),
            pltpu.VMEM((rows_dev, columns), f32),
            pltpu.VMEM((rows_dev, columns), f32),
            pltpu.VMEM((chunks, nshard, CAP, SUB, block), f32),
            [pltpu.VMEM((nshard, CAP, SUB, block), f32) for _ in range(chunks)],
            pltpu.VMEM((chunks, ndp, nx, SUB, block), f32),
            pltpu.VMEM((nbc, 128), f32),
            pltpu.VMEM((ndp, nbc, 128), f32),
            pltpu.VMEM((nbc, 128), f32),
            pltpu.VMEM((nx, nbc, 128), f32),
            dma((chunks, 4)),
            dma((chunks, 4)),
            dma((chunks, 4)),
            dma((chunks, 6)),
            dma((chunks, 6)),
            dma((chunks, nshard)),
            dma((chunks, nshard)),
            dma((chunks, ndp)),
            dma((chunks, ndp)),
            dma((ndp,)),
            dma((ndp,)),
            dma((nx,)),
            dma((nx,)),
            dma((3,)),
            dma((2,)),
        ],
        compiler_params=pltpu.CompilerParams(
            collective_id=0, has_side_effects=True, vmem_limit_bytes=58 * MIB),
    )(own, steps, grad, mom, sec)


def split(value):
    high = value.astype(jnp.bfloat16)
    low = (value - high.astype(jnp.float32)).astype(jnp.bfloat16)
    return high, low


def dot(left, right, axes=((1,), (0,))):
    return lax.dot_general(left, right, (axes, ((), ())), preferred_element_type=jnp.float32)


def product(first, second_factor):
    return dot(first[0], second_factor[0]) + (
        dot(first[0], second_factor[1]) + dot(first[1], second_factor[0]))


def mirrored(top, corner):
    half = corner.shape[0]
    return jnp.concatenate([top, jnp.concatenate([top[:, half:].T, corner], axis=1)], axis=0)


def gram(value, axes):
    cross = dot(value[0], value[1], axes)
    return dot(value[0], value[0], axes) + (cross + cross.T)


def square_of(value):
    high, low = value
    half = high.shape[0] // 2
    cross = dot(high, low)
    top = dot(high[:half], high) + (
        cross[:half] + jnp.concatenate([cross[:half, :half].T, cross[half:, :half].T], axis=1))
    corner = dot(high[half:], high[:, half:]) + (cross[half:, half:] + cross[half:, half:].T)
    return mirrored(top, corner)


def even_product(first, second_factor):
    half = first[0].shape[0] // 2
    top = product((first[0][:half], first[1][:half]), second_factor)
    corner = product(
        (first[0][half:], first[1][half:]), (second_factor[0][:, half:], second_factor[1][:, half:]))
    return mirrored(top, corner)


def owner_kernel(step_place, tab, gblk, left_prev, right_prev, mom, sec,
                 left_out, right_out, lroot_out, rroot_out, mom_out, sec_out,
                 g_ref, stat, root, mbuf, vbuf, sem, io_sem):
    taken = tab[0, step_place + 1]
    size = g_ref.shape[0]
    g_in = pltpu.make_async_copy(gblk, g_ref, sem.at[0])
    ins = [pltpu.make_async_copy(prev, stat.at[i], sem.at[1 + i])
           for i, prev in enumerate((left_prev, right_prev))]
    g_in.start()
    for copy in ins:
        copy.start()
    moves = [pltpu.make_async_copy(src, dst, io_sem.at[i])
             for i, (src, dst) in enumerate(((mom, mbuf), (sec, vbuf)))]
    for copy in moves:
        copy.start()
    g_in.wait()
    for copy in ins:
        copy.wait()
    for copy in moves:
        copy.wait()
    moves = [pltpu.make_async_copy(src, dst, io_sem.at[i])
             for i, (src, dst) in enumerate(((mbuf, mom_out), (vbuf, sec_out)))]
    for copy in moves:
        copy.start()
    stat_outs = [pltpu.make_async_copy(stat.at[i], out, sem.at[1 + i])
                 for i, out in enumerate((left_out, right_out))]
    root_outs = [pltpu.make_async_copy(root.at[i], out, sem.at[3 + i])
                 for i, out in enumerate((lroot_out, rroot_out))]
    two = range(2)

    @pl.when(taken == 0)
    def _():
        for i in two:
            stat[i] = jnp.zeros((size, size), jnp.float32)
            root[i] = jnp.zeros((size, size), jnp.float32)
            stat_outs[i].start()
            root_outs[i].start()
        for i in two:
            stat_outs[i].wait()
            root_outs[i].wait()

    @pl.when(taken != 0)
    def _():
        diagonal = lax.broadcasted_iota(jnp.int32, (size, size), 0) == lax.broadcasted_iota(
            jnp.int32, (size, size), 1)

        def complement(matrix):
            return split(jnp.where(diagonal, 1.25, 0.0) - 0.25 * matrix)

        g = split(g_ref[...])
        grams = [gram(g, axes) for axes in (((1,), (1,)), ((0,), (0,)))]
        for i in two:
            stat[i] = 0.95 * stat[i] + grams[i]
            stat_outs[i].start()
        scales, matrix = [], []
        for i in two:
            shifted = stat[i] + jnp.where(diagonal, 0.0001, 0.0)
            scale = 2.5 / jnp.sqrt(jnp.full((1, 1), jnp.sum(shifted * shifted)))
            scales.append(jnp.sqrt(jnp.sqrt(scale)))
            matrix.append(scale * shifted)
        factor = [complement(matrix[i]) for i in two]
        square = [split(square_of(factor[i])) for i in two]
        fourth = [split(square_of(square[i])) for i in two]
        matrix = [even_product(fourth[i], split(matrix[i])) for i in two]
        after = [complement(matrix[i]) for i in two]
        square = [split(square_of(after[i])) for i in two]
        current = [even_product(factor[i], after[i]) for i in two]
        fourth = [split(square_of(square[i])) for i in two]
        matrix = [even_product(fourth[i], split(matrix[i])) for i in two]
        more = tab[0, step_place] > 2
        for i in two:
            third = even_product(split(current[i]), complement(matrix[i]))
            root[i] = scales[i] * jnp.where(more, third, current[i])
            root_outs[i].start()
        for i in two:
            stat_outs[i].wait()
            root_outs[i].wait()

    for copy in moves:
        copy.wait()


def owner_step(tab, gblk, left_prev, right_prev, mom, sec, step_place):
    size = gblk.shape[0]
    f32 = jnp.float32
    square = jax.ShapeDtypeStruct((size, size), f32)
    rows = jax.ShapeDtypeStruct(mom.shape, f32)
    hbm = pl.BlockSpec(memory_space=pltpu.HBM)
    return pl.pallas_call(
        functools.partial(owner_kernel, step_place),
        out_shape=(square,) * 4 + (rows,) * 2,
        in_specs=[pl.BlockSpec(memory_space=pltpu.SMEM)] + [hbm] * 5,
        out_specs=(hbm,) * 6,
        scratch_shapes=[
            pltpu.VMEM((size, size), f32),
            pltpu.VMEM((2, size, size), f32),
            pltpu.VMEM((2, size, size), f32),
            pltpu.VMEM(mom.shape, f32),
            pltpu.VMEM(mom.shape, f32),
            pltpu.SemaphoreType.DMA((5,)),
            pltpu.SemaphoreType.DMA((2,)),
        ],
        compiler_params=pltpu.CompilerParams(vmem_limit_bytes=58 * MIB),
        cost_estimate=pl.CostEstimate(
            flops=100 * size ** 3, bytes_accessed=36 * size * size, transcendentals=0),
    )(tab, gblk, left_prev, right_prev, mom, sec)


def back_kernel(dims, block, rows_dev, tab, gblk, lroot, rroot, adam, update,
                gbuf, lbuf, rbuf, pbuf, recv2, send1, recv1, out, ad, fac, facs,
                p2_s, p2_r, f_s, f_r, p1_s, p1_r, io_sem):
    ndp, nshard, nx, nbr, nbc = dims
    _, _, o_row, o_final, _ = offsets(dims)
    me_d = lax.axis_index("dp")
    me_s = lax.axis_index("shard")
    my_x = me_s % nx
    my_row = me_s // nx
    ins = [pltpu.make_async_copy(src, dst, io_sem.at[i])
           for i, (src, dst) in enumerate(((gblk, gbuf), (rroot, rbuf), (lroot, lbuf), (adam, ad)))]
    for copy in ins:
        copy.start()
    dps = [((me_d + k) % ndp, me_s) for k in range(1, ndp)]
    shards = [(me_d, (me_s + k) % nshard) for k in range(1, nshard)]
    greet(dps + shards)
    for copy in ins:
        copy.wait()
    order = [q for q in range(nx // 2, 0, -1)] + [q for q in range(nx // 2 + 1, nx)] + [0]

    g = split(gbuf[...])
    right = split(rbuf[...])
    power = jnp.zeros((1, 1), jnp.float32)
    p2 = {}
    for q in order:
        x = (my_x + q) % nx
        span = ndp * rows_dev
        left = split(lbuf[pl.ds(pl.multiple_of(x * span, span), span), :])
        way = product(split(product(left, g)), right)
        pbuf[q] = way.reshape(ndp, rows_dev, block)
        power = power + jnp.sum(jnp.sum(way * way, axis=0, keepdims=True), axis=1, keepdims=True)
        for k in range(1, ndp):
            target = (me_d + k) % ndp
            copy = pltpu.make_async_remote_copy(
                pbuf.at[q, target], recv2[q].at[me_d], p2_s.at[q, k], p2_r.at[q, k],
                device_id=(target, me_s), device_id_type=MESH)
            copy.start()
            p2[q, k] = copy
        recv2[q][me_d] = pbuf[q, me_d]
    fac[...] = jnp.broadcast_to(1.0 / jnp.sqrt(power + 1e-12), fac.shape)
    facs[me_d] = fac[...]
    factors = []
    for k in range(1, ndp):
        copy = pltpu.make_async_remote_copy(
            fac, facs.at[me_d], f_s.at[k], f_r.at[k],
            device_id=((me_d + k) % ndp, me_s), device_id_type=MESH)
        copy.start()
        factors.append(copy)

    def scaled(q, row, j):
        rank = tab[0, o_row + row * CAP + j]
        by = jnp.concatenate([facs[rank]] * (block // 128), axis=1)
        return recv2[q][rank] * by

    p1 = {}
    for q in order:
        for k in range(1, ndp):
            p2[q, k].wait_recv()
        if q == order[0]:
            for copy in factors:
                copy.wait_recv()
        x = (my_x + q) % nx
        for w in range(nbr):
            row = (my_row + w) % nbr
            if q == 0 and w == 0:
                for j in range(CAP):
                    recv1[me_s * CAP + j] = scaled(q, row, j)
                continue
            for j in range(CAP):
                send1[q, w, j] = scaled(q, row, j)
            copy = pltpu.make_async_remote_copy(
                send1.at[q, w], recv1.at[pl.ds(me_s * CAP, CAP)], p1_s.at[q, w], p1_r.at[q, w],
                device_id=(me_d, row * nx + x), device_id_type=MESH)
            copy.start()
            p1[q, w] = copy
    for copy in p1.values():
        copy.wait_recv()
    for c in range(nbc):
        scale = jnp.concatenate([ad[pl.ds(c, 1), :]] * (block // 128), axis=1)
        out[:, pl.ds(c * block, block)] = recv1[tab[0, o_final + c]] * scale
    done = pltpu.make_async_copy(out, update, io_sem.at[0])
    done.start()
    for copy in list(p2.values()) + factors + list(p1.values()):
        copy.wait_send()
    done.wait()


def back(tab, gblk, lroot, rroot, adam, dims, block, rows_dev, columns):
    ndp, nshard, nx, nbr, nbc = dims
    f32 = jnp.float32
    hbm = pl.BlockSpec(memory_space=pltpu.HBM)
    dma = pltpu.SemaphoreType.DMA
    return pl.pallas_call(
        functools.partial(back_kernel, dims, block, rows_dev),
        out_shape=jax.ShapeDtypeStruct((rows_dev, columns), f32),
        in_specs=[pl.BlockSpec(memory_space=pltpu.SMEM)] + [hbm] * 4,
        out_specs=hbm,
        scratch_shapes=[
            pltpu.VMEM((block, block), f32),
            pltpu.VMEM((block, block), f32),
            pltpu.VMEM((block, block), f32),
            pltpu.VMEM((nx, ndp, rows_dev, block), f32),
            [pltpu.VMEM((ndp, rows_dev, block), f32) for _ in range(nx)],
            pltpu.VMEM((nx, nbr, CAP, rows_dev, block), f32),
            pltpu.VMEM((nshard * CAP, rows_dev, block), f32),
            pltpu.VMEM((rows_dev, columns), f32),
            pltpu.VMEM((nbc, 128), f32),
            pltpu.VMEM((rows_dev, 128), f32),
            pltpu.VMEM((ndp, rows_dev, 128), f32),
            dma((nx, ndp)),
            dma((nx, ndp)),
            dma((ndp,)),
            dma((ndp,)),
            dma((nx, nbr)),
            dma((nx, nbr)),
            dma((4,)),
        ],
        compiler_params=pltpu.CompilerParams(
            collective_id=1, has_side_effects=True, vmem_limit_bytes=58 * MIB),
    )(tab, gblk, lroot, rroot, adam)


def local(grad_parts, moment, second, left_prev, right_prev, owners, newton_steps):
    ndp = lax.axis_size("dp")
    nshard = lax.axis_size("shard")
    _, rows_dev, columns = moment.shape
    block = left_prev.shape[-1]
    nx = block // (rows_dev * ndp)
    dims = (ndp, nshard, nx, nshard // nx, columns // block)
    gblk, mom, sec, adam, tab = forward(
        owners[None], newton_steps[None], grad_parts[0], moment[0], second[0], dims, block)
    gblk = gblk.reshape(block, block)
    left, right, lroot, rroot, mom, sec = owner_step(
        tab, gblk, left_prev[0, 0, 0], right_prev[0, 0, 0], mom, sec, offsets(dims)[4])
    update = back(tab, gblk, lroot, rroot, adam, dims, block, rows_dev, columns)
    slots = (1, 1, 1, block, block)
    return (
        update[None],
        mom[None],
        sec[None],
        left.reshape(slots),
        right.reshape(slots),
        lroot.reshape(slots),
        rroot.reshape(slots),
    )


def solution(mesh):
    rows = P("shard", "dp", None)
    slots = P("dp", "shard", None, None, None)
    return jax.shard_map(
        local,
        mesh=mesh,
        in_specs=(P("dp", "shard", None), rows, rows, slots, slots, P(), P()),
        out_specs=(rows, rows, rows, slots, slots, slots, slots),
        check_vma=False,
    )
```

time: 123 us -> 100 us (0.81)
  Pallas kernels: 109 us -> 97.6 us
  local copies, waits for them, and re-layouts: 10.8 us -> 1.87 us
  other arithmetic: 2.63 us -> 0 us
    pallas_call x1, Pallas kernels: 33.6 us -> 14.5 us  [owner_step(): pl.pallas_call(functools.partial(owner_kernel, step_place), out_shape=(sq...]
    pallas_call x1, Pallas kernels: 27.5 us -> 35.6 us  [back(): pl.pallas_call(functools.partial(back_kernel, dims, block, rows_dev), out...]
    unnamed x19 -> x1, local copies, waits for them, and re-layouts: 9.47 us -> 1.87 us
    reduce_sum x5 -> x0, other arithmetic: 2.62 us -> none  [the longest x1 1.32 us: routes(): taken = jnp.sum(jnp.where(place, always, 0), keepdims=True)]
    concatenate x1 -> x0, local copies, waits for them, and re-layouts: 1.38 us -> none  [routes(): jnp.concatenate([sends, by_rank, by_row, finals, steps, taken])]
where the time goes in v1:
time: 100 us
  Pallas kernels  97.6 us (98%)
  local copies, waits for them, and re-layouts  1.87 us (2%)
    pallas_call x1, Pallas kernels, forward(): pl.pallas_call(body, out_shape=(jax.ShapeDtypeStruct((nx, ndp, chunks, SU...  47.5 us
    pallas_call x1, Pallas kernels, back(): pl.pallas_call(functools.partial(back_kernel, dims, block, rows_dev), out...  35.6 us
    pallas_call x1, Pallas kernels, owner_step(): pl.pallas_call(functools.partial(owner_kernel, step_place), out_shape=(sq...  14.5 us

profile of v1, /device:TPU:1, one launch (start us, length us, event | category | flops | bytes accessed | tf_op | source)
XLA Modules:
  0.0 100.1 jit_solution(7063624086089343248)
XLA Ops:
  0.6 47.5 %shard_map.126 = (f32[4,8,2,8,512]{4,3,2,1,0:T(8,128)}, f32[16,8192]{1,0:T(8,128)}, f32[16,8192]{1,0:T(8,128)}, f32[16,128]{1,0:T(8,128)}, s32[1,128]{1,0:T(1,128)}) custom-call(s32[1,64]{1,0:T(1,128)} %bitcast.23, s32[1,64]{1,0:T(1,128)} %bitcast.24, f32[128,8192]{1,0:T(8,128)} %bitcast.15, f32[16,8192]{1,0:T(8,128)} %bitcast.21, f32[16,8192]{1,0:T(8,128)} %bitcast.22), custom_call_target="tpu_custom_call" | custom-call | tf_op jit(solution)/shard_map/pallas_call | solution.py:308
  48.2 14.5 %shard_map.127 = (f32[512,512]{1,0:T(8,128)}, f32[512,512]{1,0:T(8,128)}, f32[512,512]{1,0:T(8,128)}, f32[512,512]{1,0:T(8,128)}, f32[16,8192]{1,0:T(8,128)}, /*index=5*/f32[16,8192]{1,0:T(8,128)}) custom-call(s32[1,128]{1,0:T(1,128)} %get-tuple-element.18.tab, f32[512,512]{1,0:T(8,128)} %bitcast.19, f32[512,512]{1,0:T(8,128)} %bitcast.25, ...), custom_call_target="tpu_custom_call" | custom-call | flops 13421772800 | bytes 9437184 | tf_op jit(solution)/shard_map/pallas_call | solution.py:491
  62.6 35.6 %shard_map.128 = f32[16,8192]{1,0:T(8,128)} custom-call(s32[1,128]{1,0:T(1,128)} %get-tuple-element.18.tab, f32[512,512]{1,0:T(8,128)} %bitcast.20, f32[512,512]{1,0:T(8,128)} %get-tuple-element.22.lroot, f32[512,512]{1,0:T(8,128)} %get-tuple-element.23.rroot, f32[16,128]{1,0:T(8,128)} %get-tuple-element.24.adam), custom_call_target="tpu_custom_call" | custom-call | tf_op jit(solution)/shard_map/pallas_call | solution.py:603
  98.2 1.9 %copy.15 = f32[1,16,8192]{2,1,0:T(8,128)} copy(f32[1,16,8192]{2,1,0:T(8,128)} %bitcast.16) | data formatting | bytes 1048576

commit v2 on v1

v2 whole, which is shorter than its diff:
```python
import functools

import jax
import jax.numpy as jnp
from jax import lax
from jax.experimental import pallas as pl
from jax.experimental.pallas import tpu as pltpu
from jax.sharding import PartitionSpec as P

MESH = pl.DeviceIdType.MESH
CORES = 2
LANES = 128
CAP = 2
MIB = 1 << 20


def route_table(own, steps, my_dp, my_shard, dims):
    ndp, nshard, nx, nbr, nbc = dims
    count = nbr * nbc
    o_sends, o_rank, o_row, o_final, o_steps = offsets(dims)
    down = lax.broadcasted_iota(jnp.int32, (count, count), 0)
    across = lax.broadcasted_iota(jnp.int32, (count, count), 1)
    wide = jnp.broadcast_to(own, (count, count))

    def turned(row):
        return jnp.sum(jnp.where(down == across, jnp.broadcast_to(row, (count, count)), 0), axis=1, keepdims=True)

    owner = turned(own)
    earlier = jnp.where((owner == wide) & (across < down), 1, 0)
    rank = jnp.sum(earlier, axis=1, keepdims=True)
    sub = jnp.sum(jnp.where(across // nbc == down // nbc, earlier, 0), axis=1, keepdims=True)
    count_of = turned(steps)
    lane = lax.broadcasted_iota(jnp.int32, (count, 128), 1)
    block = lax.broadcasted_iota(jnp.int32, (count, 128), 0)

    def spread(column):
        return jnp.broadcast_to(column, (count, 128))

    owner, rank, sub, count_of = (spread(column) for column in (owner, rank, sub, count_of))
    row, column = block // nbc, block % nbc
    mine = jnp.where(owner == my_shard, 1, 0)
    here = jnp.where(row == my_shard // nx, 1, 0)
    slot = owner * CAP + sub
    place = row * CAP + sub
    key = jnp.where(lane < o_rank, slot, jnp.where(lane < o_row, rank + o_rank, jnp.where(
        lane < o_final, place + o_row, jnp.where(lane < o_steps, column + o_final, -1))))
    value = jnp.where(lane < o_rank, column, jnp.where(lane < o_row, place, jnp.where(
        lane < o_final, rank, slot)))
    chosen = jnp.where((lane < o_rank) | (lane >= o_final), here, mine)
    table = jnp.where(key == lane, value * chosen, 0)
    held = jnp.where(rank == my_dp, mine, 0)
    table = table + jnp.where(lane == o_steps, held * count_of, jnp.where(lane == o_steps + 1, held, 0))
    return jnp.sum(table, axis=0, keepdims=True)


def offsets(dims):
    ndp, nshard, nx, nbr, nbc = dims
    sends = 0
    by_rank = sends + nshard * CAP
    by_row = by_rank + ndp
    finals = by_row + nbr * CAP
    steps = finals + nbc
    return sends, by_rank, by_row, finals, steps


def signal(peers):
    barrier = pltpu.get_barrier_semaphore()
    for peer in peers:
        pl.semaphore_signal(barrier, inc=1, device_id=peer, device_id_type=MESH)


def await_peers(peers):
    pl.semaphore_wait(pltpu.get_barrier_semaphore(), len(peers))


def greet(peers):
    signal(peers)
    await_peers(peers)


def joined(chunked):
    return jnp.concatenate([chunked[t] for t in range(chunked.shape[0])], axis=1)


def far_first(count, width):
    def length(k):
        across, down = k % width, k // width
        high = count // width
        return min(across, width - across) + min(down, high - down)

    return sorted(range(1, count), key=lambda k: -length(k))


def dp_steps(ndp):
    nz = ndp // CORES
    steps = [(a, c) for a in range(nz) for c in range(CORES) if a or c]
    return sorted(steps, key=lambda k: -min(k[0], nz - k[0]))


def dp_peer(me_d, step, ndp):
    nz = ndp // CORES
    return (me_d // CORES + step[0]) % nz * CORES + (me_d % CORES + step[1]) % CORES


def forward_kernel(dims, block, own, steps, grad, mom, sec,
                   gblk, mom_out, sec_out, adam_out, tab_out,
                   ibuf, tvec, tab, loc, pair, acc, first_up, first_down, from_below, from_above,
                   gsel, mbuf, vbuf, send1, recv1, send2, asend,
                   loc_sem, pair_s, pair_r, ring_s, ring_r, p1_s, p1_r, p2_s, p2_r,
                   io_sem, t_sem):
    ndp, nshard, nx, nbr, nbc = dims
    o_sends, o_rank, _, _, _ = offsets(dims)
    nz = ndp // CORES
    chunks = block // LANES
    half = nbc // 2
    rows_dev = mom.shape[0]
    me_d = lax.axis_index("dp")
    me_s = lax.axis_index("shard")
    z = me_d // CORES
    core = me_d % CORES

    def zed(step):
        return (z + step) % nz

    def rows_of(zz, cc):
        return pl.ds(pl.multiple_of((zz * CORES + cc) * rows_dev, rows_dev), rows_dev)

    order = (2, 1, nz - 1, 0)
    loads = []
    lists = [pltpu.make_async_copy(src, ibuf.at[i], t_sem.at[i]) for i, src in enumerate((own, steps))]
    for copy in lists:
        copy.start()
    for q, step in enumerate(order):
        loads.append(pltpu.make_async_copy(
            grad.at[rows_of(zed(step), core), :], loc.at[q], loc_sem.at[q]))
        loads[q].start()
    m_in = pltpu.make_async_copy(mom, mbuf, io_sem.at[0])
    v_in = pltpu.make_async_copy(sec, vbuf, io_sem.at[1])
    m_in.start()
    v_in.start()

    z_steps = dp_steps(ndp)
    s_steps = far_first(nshard, nx)
    greet([(dp_peer(me_d, step, ndp), me_s) for step in z_steps]
          + [(me_d, shard_peer(me_s, k, dims)) for k in s_steps])

    sibling = (z * CORES + (1 - core), me_s)
    above = (zed(1) * CORES + core, me_s)
    below = (zed(nz - 1) * CORES + core, me_s)
    pairs = []
    for q, step in enumerate(order):
        pairs.append(pltpu.make_async_remote_copy(
            grad.at[rows_of(zed(step), 1 - core), :], pair.at[q],
            pair_s.at[q], pair_r.at[q], device_id=sibling, device_id_type=MESH))
        pairs[q].start()

    for copy in lists:
        copy.wait()
    tvec[...] = route_table(ibuf[0], ibuf[1], me_d, me_s, dims)
    table_in = pltpu.make_async_copy(tvec, tab, t_sem.at[0])
    table_in.start()
    table_out = pltpu.make_async_copy(tvec, tab_out, t_sem.at[1])
    table_out.start()

    lo = pl.ds(0, half)
    hi = pl.ds(half, half)
    ring = {}

    def ring_send(t, index, src, dst, target):
        copy = pltpu.make_async_remote_copy(
            src, dst, ring_s.at[t, index], ring_r.at[t, index], device_id=target, device_id_type=MESH)
        copy.start()
        ring[t, index] = copy

    def merge(t, q):
        if t == 0:
            loads[q].wait()
            pairs[q].wait_recv()
        for c in range(nbc):
            cols = pl.ds(c * block + t * LANES, LANES)
            acc[t, q, c] = loc[q, :, cols] + pair[q, :, cols]

    def ring_one(t):
        merge(t, 0)
        ring_send(t, 0, acc.at[t, 0, lo], first_up.at[t], above)
        ring_send(t, 1, acc.at[t, 0, hi], first_down.at[t], below)
        merge(t, 1)
        ring_send(t, 2, acc.at[t, 1, hi], from_below.at[t, hi], above)
        merge(t, 2)
        ring_send(t, 3, acc.at[t, 2, lo], from_above.at[t, lo], below)
        merge(t, 3)

    def ring_two(t):
        ring[t, 0].wait_recv()
        acc[t, 1, lo] = acc[t, 1, lo] + first_up[t]
        ring_send(t, 4, acc.at[t, 1, lo], from_below.at[t, lo], above)
        ring[t, 1].wait_recv()
        acc[t, 2, hi] = acc[t, 2, hi] + first_down[t]
        ring_send(t, 5, acc.at[t, 2, hi], from_above.at[t, hi], below)

    def ring_end(t):
        for index in range(2, 6):
            ring[t, index].wait_recv()
        gsel[t] = (acc[t, 3] + from_below[t]) + from_above[t]

    p1 = {}

    def exchange_shards(t):
        for k in s_steps:
            target = shard_peer(me_s, k, dims)
            for j in range(CAP):
                send1[t, k, j] = gsel[t, tab[0, o_sends + target * CAP + j]]
            copy = pltpu.make_async_remote_copy(
                send1.at[t, k], recv1[t].at[me_s], p1_s.at[t, k], p1_r.at[t, k],
                device_id=(me_d, target), device_id_type=MESH)
            copy.start()
            p1[t, k] = copy
        for j in range(CAP):
            recv1[t][me_s, j] = gsel[t, tab[0, o_sends + me_s * CAP + j]]

    p2 = {}

    def exchange_dp(t):
        for k in s_steps:
            p1[t, k].wait_recv()
        for k, step in enumerate(z_steps + [(0, 0)]):
            target = dp_peer(me_d, step, ndp)
            place = tab[0, o_rank + target]
            r = place // CAP
            j = place % CAP
            for x in range(nx):
                send2[t, k, x] = recv1[t][r * nx + x, j]
            if k < len(z_steps):
                copy = pltpu.make_async_remote_copy(
                    send2.at[t, k], gblk.at[t, :, me_d], p2_s.at[t, k], p2_r.at[t, k],
                    device_id=(target, me_s), device_id_type=MESH)
            else:
                copy = pltpu.make_async_copy(send2.at[t, k], gblk.at[t, :, me_d], p2_s.at[t, k])
            copy.start()
            p2[t, k] = copy

    def adam_rows(t):
        for c in range(nbc):
            cols = pl.ds(c * block + t * LANES, LANES)
            g = gsel[t, c]
            m = 0.9 * mbuf[:, cols] + 0.1 * g
            v = 0.99 * vbuf[:, cols] + 0.01 * g * g
            mbuf[:, cols] = m
            vbuf[:, cols] = v
            a = m / (jnp.sqrt(v) + 1e-08)
            part = jnp.sum(a * a, axis=0, keepdims=True)
            if t == 0:
                asend[pl.ds(c, 1), :] = part
            else:
                asend[pl.ds(c, 1), :] = asend[pl.ds(c, 1), :] + part

    def shards_out(t):
        if t == 0:
            table_in.wait()
        ring_end(t)
        exchange_shards(t)

    ring_one(0)
    for t in range(1, chunks):
        ring_one(t)
        ring_two(t - 1)
        if t >= 2:
            shards_out(t - 2)
    ring_two(chunks - 1)
    for t in range(max(chunks - 2, 0), chunks):
        shards_out(t)
        if t > max(chunks - 2, 0):
            exchange_dp(t - (chunks - 1))
    m_in.wait()
    v_in.wait()
    for t in range(chunks):
        adam_rows(t)
        if t + 1 < chunks:
            exchange_dp(t + 1)

    m_out = pltpu.make_async_copy(mbuf, mom_out, io_sem.at[0])
    v_out = pltpu.make_async_copy(vbuf, sec_out, io_sem.at[1])
    a_out = pltpu.make_async_copy(asend, adam_out, io_sem.at[2])
    for copy in (m_out, v_out, a_out):
        copy.start()

    for copy in pairs + list(ring.values()) + list(p1.values()):
        copy.wait_send()
    for (t, k), copy in p2.items():
        if k < len(z_steps):
            copy.wait_send()
            copy.wait_recv()
        else:
            copy.wait()
    m_out.wait()
    v_out.wait()
    a_out.wait()
    table_out.wait()


def shard_peer(me_s, k, dims):
    _, _, nx, nbr, _ = dims
    return (me_s // nx + k // nx) % nbr * nx + (me_s % nx + k % nx) % nx


def forward(own, steps, grad, mom, sec, dims, block):
    ndp, nshard, nx, nbr, nbc = dims
    rows_dev, columns = mom.shape
    chunks = block // LANES
    f32 = jnp.float32
    hbm = pl.BlockSpec(memory_space=pltpu.HBM)
    dma = pltpu.SemaphoreType.DMA
    piece = (rows_dev, LANES)
    return pl.pallas_call(
        functools.partial(forward_kernel, dims, block),
        out_shape=(
            jax.ShapeDtypeStruct((chunks, nx, ndp) + piece, f32),
            jax.ShapeDtypeStruct((rows_dev, columns), f32),
            jax.ShapeDtypeStruct((rows_dev, columns), f32),
            jax.ShapeDtypeStruct((nbc, LANES), f32),
            jax.ShapeDtypeStruct((1, LANES), jnp.int32),
        ),
        in_specs=[hbm] * 5,
        out_specs=(hbm,) * 5,
        scratch_shapes=[
            pltpu.VMEM((2, 1, nbr * nbc), jnp.int32),
            pltpu.VMEM((1, LANES), jnp.int32),
            pltpu.SMEM((1, LANES), jnp.int32),
            pltpu.VMEM((4, rows_dev, columns), f32),
            pltpu.VMEM((4, rows_dev, columns), f32),
            pltpu.VMEM((chunks, 4, nbc) + piece, f32),
            pltpu.VMEM((chunks, nbc // 2) + piece, f32),
            pltpu.VMEM((chunks, nbc // 2) + piece, f32),
            pltpu.VMEM((chunks, nbc) + piece, f32),
            pltpu.VMEM((chunks, nbc) + piece, f32),
            pltpu.VMEM((chunks, nbc) + piece, f32),
            pltpu.VMEM((rows_dev, columns), f32),
            pltpu.VMEM((rows_dev, columns), f32),
            pltpu.VMEM((chunks, nshard, CAP) + piece, f32),
            [pltpu.VMEM((nshard, CAP) + piece, f32) for _ in range(chunks)],
            pltpu.VMEM((chunks, ndp, nx) + piece, f32),
            pltpu.VMEM((nbc, LANES), f32),
            dma((4,)),
            dma((4,)),
            dma((4,)),
            dma((chunks, 6)),
            dma((chunks, 6)),
            dma((chunks, nshard)),
            dma((chunks, nshard)),
            dma((chunks, ndp)),
            dma((chunks, ndp)),
            dma((3,)),
            dma((2,)),
        ],
        compiler_params=pltpu.CompilerParams(
            collective_id=0, has_side_effects=True, vmem_limit_bytes=58 * MIB),
    )(own, steps, grad, mom, sec)


def split(value):
    high = value.astype(jnp.bfloat16)
    low = (value - high.astype(jnp.float32)).astype(jnp.bfloat16)
    return high, low


def dot(left, right, axes=((1,), (0,))):
    return lax.dot_general(left, right, (axes, ((), ())), preferred_element_type=jnp.float32)


def product(first, second_factor):
    return dot(first[0], second_factor[0]) + (
        dot(first[0], second_factor[1]) + dot(first[1], second_factor[0]))


def mirrored(top, corner):
    half = corner.shape[0]
    return jnp.concatenate([top, jnp.concatenate([top[:, half:].T, corner], axis=1)], axis=0)


def gram(value, axes):
    cross = dot(value[0], value[1], axes)
    return dot(value[0], value[0], axes) + (cross + cross.T)


def square_of(value):
    high, low = value
    half = high.shape[0] // 2
    cross = dot(high, low)
    top = dot(high[:half], high) + (
        cross[:half] + jnp.concatenate([cross[:half, :half].T, cross[half:, :half].T], axis=1))
    corner = dot(high[half:], high[:, half:]) + (cross[half:, half:] + cross[half:, half:].T)
    return mirrored(top, corner)


def even_product(first, second_factor):
    half = first[0].shape[0] // 2
    top = product((first[0][:half], first[1][:half]), second_factor)
    corner = product(
        (first[0][half:], first[1][half:]), (second_factor[0][:, half:], second_factor[1][:, half:]))
    return mirrored(top, corner)


def owner_kernel(step_place, tab, gblk, left_prev, right_prev, mom, sec,
                 left_out, right_out, lroot_out, rroot_out, mom_out, sec_out,
                 g_ref, stat, root, mbuf, vbuf, sem, io_sem):
    taken = tab[0, step_place + 1]
    size = g_ref.shape[1]
    g_in = pltpu.make_async_copy(gblk, g_ref, sem.at[0])
    ins = [pltpu.make_async_copy(prev, stat.at[i], sem.at[1 + i])
           for i, prev in enumerate((left_prev, right_prev))]
    g_in.start()
    for copy in ins:
        copy.start()
    moves = [pltpu.make_async_copy(src, dst, io_sem.at[i])
             for i, (src, dst) in enumerate(((mom, mbuf), (sec, vbuf)))]
    for copy in moves:
        copy.start()
    g_in.wait()
    for copy in ins:
        copy.wait()
    for copy in moves:
        copy.wait()
    moves = [pltpu.make_async_copy(src, dst, io_sem.at[i])
             for i, (src, dst) in enumerate(((mbuf, mom_out), (vbuf, sec_out)))]
    for copy in moves:
        copy.start()
    stat_outs = [pltpu.make_async_copy(stat.at[i], out, sem.at[1 + i])
                 for i, out in enumerate((left_out, right_out))]
    root_outs = [pltpu.make_async_copy(root.at[i], out, sem.at[3 + i])
                 for i, out in enumerate((lroot_out, rroot_out))]
    two = range(2)

    @pl.when(taken == 0)
    def _():
        for i in two:
            stat[i] = jnp.zeros((size, size), jnp.float32)
            root[i] = jnp.zeros((size, size), jnp.float32)
            stat_outs[i].start()
            root_outs[i].start()
        for i in two:
            stat_outs[i].wait()
            root_outs[i].wait()

    @pl.when(taken != 0)
    def _():
        diagonal = lax.broadcasted_iota(jnp.int32, (size, size), 0) == lax.broadcasted_iota(
            jnp.int32, (size, size), 1)

        def complement(matrix):
            return split(jnp.where(diagonal, 1.25, 0.0) - 0.25 * matrix)

        g = split(joined(g_ref))
        grams = [gram(g, axes) for axes in (((1,), (1,)), ((0,), (0,)))]
        for i in two:
            stat[i] = 0.95 * stat[i] + grams[i]
            stat_outs[i].start()
        scales, matrix = [], []
        for i in two:
            shifted = stat[i] + jnp.where(diagonal, 0.0001, 0.0)
            scale = 2.5 / jnp.sqrt(jnp.full((1, 1), jnp.sum(shifted * shifted)))
            scales.append(jnp.sqrt(jnp.sqrt(scale)))
            matrix.append(scale * shifted)
        factor = [complement(matrix[i]) for i in two]
        square = [split(square_of(factor[i])) for i in two]
        fourth = [split(square_of(square[i])) for i in two]
        matrix = [even_product(fourth[i], split(matrix[i])) for i in two]
        after = [complement(matrix[i]) for i in two]
        square = [split(square_of(after[i])) for i in two]
        current = [even_product(factor[i], after[i]) for i in two]
        fourth = [split(square_of(square[i])) for i in two]
        matrix = [even_product(fourth[i], split(matrix[i])) for i in two]
        more = tab[0, step_place] > 2
        for i in two:
            third = even_product(split(current[i]), complement(matrix[i]))
            root[i] = scales[i] * jnp.where(more, third, current[i])
            root_outs[i].start()
        for i in two:
            stat_outs[i].wait()
            root_outs[i].wait()

    for copy in moves:
        copy.wait()


def owner_step(tab, gblk, left_prev, right_prev, mom, sec, step_place):
    size = gblk.shape[1]
    f32 = jnp.float32
    square = jax.ShapeDtypeStruct((size, size), f32)
    rows = jax.ShapeDtypeStruct(mom.shape, f32)
    hbm = pl.BlockSpec(memory_space=pltpu.HBM)
    return pl.pallas_call(
        functools.partial(owner_kernel, step_place),
        out_shape=(square,) * 4 + (rows,) * 2,
        in_specs=[pl.BlockSpec(memory_space=pltpu.SMEM)] + [hbm] * 5,
        out_specs=(hbm,) * 6,
        scratch_shapes=[
            pltpu.VMEM(gblk.shape, f32),
            pltpu.VMEM((2, size, size), f32),
            pltpu.VMEM((2, size, size), f32),
            pltpu.VMEM(mom.shape, f32),
            pltpu.VMEM(mom.shape, f32),
            pltpu.SemaphoreType.DMA((5,)),
            pltpu.SemaphoreType.DMA((2,)),
        ],
        compiler_params=pltpu.CompilerParams(vmem_limit_bytes=58 * MIB),
        cost_estimate=pl.CostEstimate(
            flops=100 * size ** 3, bytes_accessed=36 * size * size, transcendentals=0),
    )(tab, gblk, left_prev, right_prev, mom, sec)


def back_kernel(dims, block, rows_dev, tab, gblk, lroot, rroot, adam, update,
                gbuf, lbuf, rbuf, pbuf, recv2, send1, recv1, out, asend, arecv, xsend, xrecv,
                p2_s, p2_r, a_s, a_r, x_s, x_r, p1_s, p1_r, io_sem):
    ndp, nshard, nx, nbr, nbc = dims
    _, _, o_row, o_final, _ = offsets(dims)
    chunks = block // LANES
    me_d = lax.axis_index("dp")
    me_s = lax.axis_index("shard")
    ins = [pltpu.make_async_copy(src, dst, io_sem.at[i])
           for i, (src, dst) in enumerate(((lroot, lbuf), (gblk, gbuf), (rroot, rbuf), (adam, asend)))]
    for copy in ins:
        copy.start()
    z_steps = dp_steps(ndp)
    s_steps = far_first(nshard, nx)
    peers = [(dp_peer(me_d, step, ndp), me_s) for step in z_steps] + [
        (me_d, shard_peer(me_s, k, dims)) for k in s_steps]
    signal(peers)
    for copy in ins:
        copy.wait()
    turned = split(product(split(lbuf[...]), split(joined(gbuf))))
    way = product(turned, split(rbuf[...]))
    power = jnp.sum(jnp.sum(way * way, axis=0, keepdims=True), axis=1, keepdims=True)
    way = way * (1.0 / jnp.sqrt(power + 1e-12))
    for t in range(chunks):
        for x in range(nx):
            for d in range(ndp):
                top = (x * ndp + d) * rows_dev
                pbuf[t, d, x] = way[top:top + rows_dev, t * LANES:(t + 1) * LANES]
    await_peers(peers)

    acopies = []
    for k, step in enumerate(z_steps):
        copy = pltpu.make_async_remote_copy(
            asend, arecv.at[k], a_s.at[k], a_r.at[k],
            device_id=(dp_peer(me_d, step, ndp), me_s), device_id_type=MESH)
        copy.start()
        acopies.append(copy)
    p2 = {}
    for t in range(chunks):
        for k, step in enumerate(z_steps):
            target = dp_peer(me_d, step, ndp)
            copy = pltpu.make_async_remote_copy(
                pbuf.at[t, target], recv2[t].at[me_d], p2_s.at[t, k], p2_r.at[t, k],
                device_id=(target, me_s), device_id_type=MESH)
            copy.start()
            p2[t, k] = copy
        recv2[t][me_d] = pbuf[t, me_d]
    total = asend[...]
    for k, copy in enumerate(acopies):
        copy.wait_recv()
        total = total + arecv[k]
    xsend[...] = total
    xcopies = []
    for k in range(1, nx):
        copy = pltpu.make_async_remote_copy(
            xsend, xrecv.at[k], x_s.at[k], x_r.at[k],
            device_id=(me_d, me_s // nx * nx + (me_s % nx + k) % nx), device_id_type=MESH)
        copy.start()
        xcopies.append(copy)

    p1 = {}
    for t in range(chunks):
        for k in range(len(z_steps)):
            p2[t, k].wait_recv()

        def wanted(target, j):
            rank = tab[0, o_row + target // nx * CAP + j]
            return recv2[t][rank, target % nx]

        for k in s_steps:
            target = shard_peer(me_s, k, dims)
            for j in range(CAP):
                send1[t, k, j] = wanted(target, j)
            copy = pltpu.make_async_remote_copy(
                send1.at[t, k], recv1[t].at[pl.ds(me_s * CAP, CAP)], p1_s.at[t, k], p1_r.at[t, k],
                device_id=(me_d, target), device_id_type=MESH)
            copy.start()
            p1[t, k] = copy
        for j in range(CAP):
            recv1[t][me_s * CAP + j] = wanted(me_s, j)
    for k in range(1, nx):
        xcopies[k - 1].wait_recv()
        total = total + xrecv[k]
    ad = jnp.broadcast_to(jnp.sqrt(jnp.sum(total, axis=1, keepdims=True)), total.shape)
    for t in range(chunks):
        for k in s_steps:
            p1[t, k].wait_recv()
        for c in range(nbc):
            cols = pl.ds(c * block + t * LANES, LANES)
            out[:, cols] = recv1[t][tab[0, o_final + c]] * ad[c:c + 1, :]
    done = pltpu.make_async_copy(out, update, io_sem.at[0])
    done.start()
    for copy in list(p2.values()) + acopies + xcopies + list(p1.values()):
        copy.wait_send()
    done.wait()


def back(tab, gblk, lroot, rroot, adam, dims, block, rows_dev, columns):
    ndp, nshard, nx, nbr, nbc = dims
    chunks = block // LANES
    f32 = jnp.float32
    hbm = pl.BlockSpec(memory_space=pltpu.HBM)
    dma = pltpu.SemaphoreType.DMA
    piece = (rows_dev, LANES)
    return pl.pallas_call(
        functools.partial(back_kernel, dims, block, rows_dev),
        out_shape=jax.ShapeDtypeStruct((rows_dev, columns), f32),
        in_specs=[pl.BlockSpec(memory_space=pltpu.SMEM)] + [hbm] * 4,
        out_specs=pl.BlockSpec(memory_space=pl.ANY),
        scratch_shapes=[
            pltpu.VMEM(gblk.shape, f32),
            pltpu.VMEM((block, block), f32),
            pltpu.VMEM((block, block), f32),
            pltpu.VMEM((chunks, ndp, nx) + piece, f32),
            [pltpu.VMEM((ndp, nx) + piece, f32) for _ in range(chunks)],
            pltpu.VMEM((chunks, nshard, CAP) + piece, f32),
            [pltpu.VMEM((nshard * CAP,) + piece, f32) for _ in range(chunks)],
            pltpu.VMEM((rows_dev, columns), f32),
            pltpu.VMEM((nbc, LANES), f32),
            pltpu.VMEM((ndp, nbc, LANES), f32),
            pltpu.VMEM((nbc, LANES), f32),
            pltpu.VMEM((nx, nbc, LANES), f32),
            dma((chunks, ndp)),
            dma((chunks, ndp)),
            dma((ndp,)),
            dma((ndp,)),
            dma((nx,)),
            dma((nx,)),
            dma((chunks, nshard)),
            dma((chunks, nshard)),
            dma((4,)),
        ],
        compiler_params=pltpu.CompilerParams(
            collective_id=1, has_side_effects=True, vmem_limit_bytes=63 * MIB),
    )(tab, gblk, lroot, rroot, adam)


def local(grad_parts, moment, second, left_prev, right_prev, owners, newton_steps):
    ndp = lax.axis_size("dp")
    nshard = lax.axis_size("shard")
    _, rows_dev, columns = moment.shape
    block = left_prev.shape[-1]
    nx = block // (rows_dev * ndp)
    dims = (ndp, nshard, nx, nshard // nx, columns // block)
    gblk, mom, sec, adam, tab = forward(
        owners[None], newton_steps[None], grad_parts[0], moment[0], second[0], dims, block)
    gblk = gblk.reshape(block // LANES, block, LANES)
    left, right, lroot, rroot, mom, sec = owner_step(
        tab, gblk, left_prev[0, 0, 0], right_prev[0, 0, 0], mom, sec, offsets(dims)[4])
    update = back(tab, gblk, lroot, rroot, adam, dims, block, rows_dev, columns)
    slots = (1, 1, 1, block, block)
    return (
        update[None],
        mom[None],
        sec[None],
        left.reshape(slots),
        right.reshape(slots),
        lroot.reshape(slots),
        rroot.reshape(slots),
    )


def solution(mesh):
    rows = P("shard", "dp", None)
    slots = P("dp", "shard", None, None, None)
    return jax.shard_map(
        local,
        mesh=mesh,
        in_specs=(P("dp", "shard", None), rows, rows, slots, slots, P(), P()),
        out_specs=(rows, rows, rows, slots, slots, slots, slots),
        check_vma=False,
    )
```

time: 100 us -> 90.6 us (0.906)
  Pallas kernels: 97.6 us -> 87.9 us
    pallas_call x1, Pallas kernels: 35.6 us -> 26.6 us  [back(): pl.pallas_call(functools.partial(back_kernel, dims, block, rows_dev), out...]
where the time goes in v2:
time: 90.6 us; the launch traced here: 90.4 us
  Pallas kernels  87.9 us (97%)
  local copies, waits for them, and re-layouts  1.87 us (2%)
    pallas_call x1, Pallas kernels, forward(): pl.pallas_call(functools.partial(forward_kernel, dims, block), out_shape=...  46.9 us
    pallas_call x1, Pallas kernels, back(): pl.pallas_call(functools.partial(back_kernel, dims, block, rows_dev), out...  26.6 us
    pallas_call x1, Pallas kernels, owner_step(): pl.pallas_call(functools.partial(owner_kernel, step_place), out_shape=(sq...  14.5 us
    unnamed x1, local copies, waits for them, and re-layouts  1.87 us

profile of v2, /device:TPU:1, one launch (start us, length us, event | category | flops | bytes accessed | tf_op | source)
XLA Modules:
  0.0 90.4 jit_solution(75254498798574981)
XLA Ops:
  0.6 46.9 %shard_map.126 = (f32[4,4,8,16,128]{4,3,2,1,0:T(8,128)}, f32[16,8192]{1,0:T(8,128)}, f32[16,8192]{1,0:T(8,128)}, f32[16,128]{1,0:T(8,128)}, s32[1,128]{1,0:T(1,128)}) custom-call(s32[1,64]{1,0:T(1,128)} %bitcast.23, s32[1,64]{1,0:T(1,128)} %bitcast.24, f32[128,8192]{1,0:T(8,128)} %bitcast.15, f32[16,8192]{1,0:T(8,128)} %bitcast.21, f32[16,8192]{1,0:T(8,128)} %bitcast.22), custom_call_target="tpu_custom_call" | custom-call | tf_op jit(solution)/shard_map/pallas_call | solution.py:314
  47.5 14.5 %shard_map.127 = (f32[512,512]{1,0:T(8,128)}, f32[512,512]{1,0:T(8,128)}, f32[512,512]{1,0:T(8,128)}, f32[512,512]{1,0:T(8,128)}, f32[16,8192]{1,0:T(8,128)}, /*index=5*/f32[16,8192]{1,0:T(8,128)}) custom-call(s32[1,128]{1,0:T(1,128)} %get-tuple-element.18.tab, f32[4,512,128]{2,1,0:T(8,128)} %bitcast.19, f32[512,512]{1,0:T(8,128)} %bitcast.25, ...), custom_call_target="tpu_custom_call" | custom-call | flops 13421772800 | bytes 9437184 | tf_op jit(solution)/shard_map/pallas_call | solution.py:491
  62.0 26.6 %shard_map.128 = f32[16,8192]{1,0:T(8,128)} custom-call(s32[1,128]{1,0:T(1,128)} %get-tuple-element.18.tab, f32[4,512,128]{2,1,0:T(8,128)} %bitcast.20, f32[512,512]{1,0:T(8,128)} %get-tuple-element.22.lroot, f32[512,512]{1,0:T(8,128)} %get-tuple-element.23.rroot, f32[16,128]{1,0:T(8,128)} %get-tuple-element.24.adam), custom_call_target="tpu_custom_call" | custom-call | tf_op jit(solution)/shard_map/pallas_call | solution.py:615
  88.6 1.9 %copy.15 = f32[1,16,8192]{2,1,0:T(8,128)} copy(f32[1,16,8192]{2,1,0:T(8,128)} %bitcast.16) | data formatting | bytes 1048576

commit v3 on v2

--- a/solution.py
+++ b/solution.py
@@ -141,7 +141,7 @@
 
     z_steps = dp_steps(ndp)
     s_steps = far_first(nshard, nx)
-    greet([(dp_peer(me_d, step, ndp), me_s) for step in z_steps]
+    greet([(dp_peer(me_d, step, ndp), me_s) for step in reversed(z_steps)]
           + [(me_d, shard_peer(me_s, k, dims)) for k in s_steps])
 
     sibling = (z * CORES + (1 - core), me_s)
@@ -153,14 +153,6 @@
             grad.at[rows_of(zed(step), 1 - core), :], pair.at[q],
             pair_s.at[q], pair_r.at[q], device_id=sibling, device_id_type=MESH))
         pairs[q].start()
-
-    for copy in lists:
-        copy.wait()
-    tvec[...] = route_table(ibuf[0], ibuf[1], me_d, me_s, dims)
-    table_in = pltpu.make_async_copy(tvec, tab, t_sem.at[0])
-    table_in.start()
-    table_out = pltpu.make_async_copy(tvec, tab_out, t_sem.at[1])
-    table_out.start()
 
     lo = pl.ds(0, half)
     hi = pl.ds(half, half)
@@ -255,28 +247,48 @@
                 asend[pl.ds(c, 1), :] = asend[pl.ds(c, 1), :] + part
 
     def shards_out(t):
-        if t == 0:
-            table_in.wait()
         ring_end(t)
         exchange_shards(t)
 
     ring_one(0)
     for t in range(1, chunks):
         ring_one(t)
+        if t == 1:
+            for copy in lists:
+                copy.wait()
+            tvec[...] = route_table(ibuf[0], ibuf[1], me_d, me_s, dims)
+            table_in = pltpu.make_async_copy(tvec, tab, t_sem.at[0])
+            table_in.start()
+            table_out = pltpu.make_async_copy(tvec, tab_out, t_sem.at[1])
+            table_out.start()
         ring_two(t - 1)
+        if t == 1:
+            table_in.wait()
         if t >= 2:
             shards_out(t - 2)
     ring_two(chunks - 1)
-    for t in range(max(chunks - 2, 0), chunks):
-        shards_out(t)
-        if t > max(chunks - 2, 0):
-            exchange_dp(t - (chunks - 1))
     m_in.wait()
     v_in.wait()
-    for t in range(chunks):
-        adam_rows(t)
-        if t + 1 < chunks:
-            exchange_dp(t + 1)
+    sent = 0
+    for t in range(max(chunks - 2, 0), chunks):
+        if sent < t:
+            exchange_dp(sent)
+            sent += 1
+        shards_out(t)
+    done = 0
+    while sent < chunks:
+        if sent < chunks - 2:
+            exchange_dp(sent)
+            sent += 1
+        for _ in range(2):
+            if done < chunks:
+                adam_rows(done)
+                done += 1
+        exchange_dp(sent)
+        sent += 1
+    while done < chunks:
+        adam_rows(done)
+        done += 1
 
     m_out = pltpu.make_async_copy(mbuf, mom_out, io_sem.at[0])
     v_out = pltpu.make_async_copy(vbuf, sec_out, io_sem.at[1])
@@ -641,7 +653,7 @@
             dma((4,)),
         ],
         compiler_params=pltpu.CompilerParams(
-            collective_id=1, has_side_effects=True, vmem_limit_bytes=63 * MIB),
+            collective_id=1, has_side_effects=True, vmem_limit_bytes=53 * MIB),
     )(tab, gblk, lroot, rroot, adam)
 
 

time: 90.6 us -> 87.2 us (0.962)
  Pallas kernels: 87.9 us -> 85.6 us
  local copies, waits for them, and re-layouts: 1.87 us -> 0.8 us
    pallas_call x1, Pallas kernels: 46.9 us -> 44.4 us  [forward(): pl.pallas_call(functools.partial(forward_kernel, dims, block), out_shape=...]
    unnamed x1 -> x5, local copies, waits for them, and re-layouts: 1.87 us -> 0.8 us
where the time goes in v3:
time: 87.2 us; the launch traced here: 87.1 us
  Pallas kernels  85.6 us (98%)
    pallas_call x1, Pallas kernels, forward(): pl.pallas_call(functools.partial(forward_kernel, dims, block), out_shape=...  44.4 us
    pallas_call x1, Pallas kernels, back(): pl.pallas_call(functools.partial(back_kernel, dims, block, rows_dev), out...  26.7 us
    pallas_call x1, Pallas kernels, owner_step(): pl.pallas_call(functools.partial(owner_kernel, step_place), out_shape=(sq...  14.5 us

profile of v3, /device:TPU:1, one launch (start us, length us, event | category | flops | bytes accessed | tf_op | source)
XLA Modules:
  0.0 87.1 jit_solution(6087119498823062004)
XLA Ops:
  0.6 44.4 %shard_map.126 = (f32[4,4,8,16,128]{4,3,2,1,0:T(8,128)}, f32[16,8192]{1,0:T(8,128)}, f32[16,8192]{1,0:T(8,128)}, f32[16,128]{1,0:T(8,128)}, s32[1,128]{1,0:T(1,128)}) custom-call(s32[1,64]{1,0:T(1,128)} %bitcast.23, s32[1,64]{1,0:T(1,128)} %bitcast.24, f32[128,8192]{1,0:T(8,128)} %bitcast.16, f32[16,8192]{1,0:T(8,128)} %bitcast.21, f32[16,8192]{1,0:T(8,128)} %bitcast.22), custom_call_target="tpu_custom_call" | custom-call | tf_op jit(solution)/shard_map/pallas_call | solution.py:326
  45.0 0.0 copy-start
  45.0 0.0 copy-start.1
  45.0 14.5 %shard_map.127 = (f32[512,512]{1,0:T(8,128)}, f32[512,512]{1,0:T(8,128)}, f32[512,512]{1,0:T(8,128)}, f32[512,512]{1,0:T(8,128)}, f32[16,8192]{1,0:T(8,128)}, /*index=5*/f32[16,8192]{1,0:T(8,128)}) custom-call(s32[1,128]{1,0:T(1,128)} %get-tuple-element.18.tab, f32[4,512,128]{2,1,0:T(8,128)} %bitcast.19, f32[512,512]{1,0:T(8,128)} %bitcast.25, ...), custom_call_target="tpu_custom_call" | custom-call | flops 13421772800 | bytes 9437184 | tf_op jit(solution)/shard_map/pallas_call | solution.py:503
  59.5 0.0 copy-done
  59.5 0.0 copy-done.1
  59.6 26.7 %shard_map.128 = f32[16,8192]{1,0:T(8,128)S(1)} custom-call(s32[1,128]{1,0:T(1,128)S(1)} %copy-done.1, f32[4,512,128]{2,1,0:T(8,128)} %bitcast.20, f32[512,512]{1,0:T(8,128)} %get-tuple-element.22.lroot, f32[512,512]{1,0:T(8,128)} %get-tuple-element.23.rroot, f32[16,128]{1,0:T(8,128)S(1)} %copy-done), custom_call_target="tpu_custom_call" | custom-call | tf_op jit(solution)/shard_map/pallas_call | solution.py:627
  86.3 0.8 copy.15
Async XLA Ops:
  45.0 14.5 %copy-start = (f32[16,128]{1,0:T(8,128)S(1)}, f32[16,128]{1,0:T(8,128)}, u32[]{:S(2)}) copy-start(f32[16,128]{1,0:T(8,128)} %get-tuple-element.24.adam) | copy-start | bytes 24580
  45.0 14.5 %copy-start.1 = (s32[1,128]{1,0:T(1,128)S(1)}, s32[1,128]{1,0:T(1,128)}, u32[]{:S(2)}) copy-start(s32[1,128]{1,0:T(1,128)} %get-tuple-element.18.tab) | copy-start | bytes 1540

commit v4 on v3

--- a/solution.py
+++ b/solution.py
@@ -104,9 +104,9 @@
 
 def forward_kernel(dims, block, own, steps, grad, mom, sec,
                    gblk, mom_out, sec_out, adam_out, tab_out,
-                   ibuf, tvec, tab, loc, pair, acc, first_up, first_down, from_below, from_above,
+                   ibuf, tvec, tab, loc, pair, other, raw, crossed, acc, first_up, first_down, from_below, from_above,
                    gsel, mbuf, vbuf, send1, recv1, send2, asend,
-                   loc_sem, pair_s, pair_r, ring_s, ring_r, p1_s, p1_r, p2_s, p2_r,
+                   loc_sem, pair_s, pair_r, cross_s, cross_r, ring_s, ring_r, p1_s, p1_r, p2_s, p2_r,
                    io_sem, t_sem):
     ndp, nshard, nx, nbr, nbc = dims
     o_sends, o_rank, _, _, _ = offsets(dims)
@@ -133,11 +133,11 @@
     for q, step in enumerate(order):
         loads.append(pltpu.make_async_copy(
             grad.at[rows_of(zed(step), core), :], loc.at[q], loc_sem.at[q]))
-        loads[q].start()
+    other_in = pltpu.make_async_copy(grad.at[rows_of(zed(order[0]), 1 - core), :], other, t_sem.at[2])
+    loads[0].start()
+    other_in.start()
     m_in = pltpu.make_async_copy(mom, mbuf, io_sem.at[0])
     v_in = pltpu.make_async_copy(sec, vbuf, io_sem.at[1])
-    m_in.start()
-    v_in.start()
 
     z_steps = dp_steps(ndp)
     s_steps = far_first(nshard, nx)
@@ -152,11 +152,14 @@
         pairs.append(pltpu.make_async_remote_copy(
             grad.at[rows_of(zed(step), 1 - core), :], pair.at[q],
             pair_s.at[q], pair_r.at[q], device_id=sibling, device_id_type=MESH))
-        pairs[q].start()
+    pairs[0].start()
+    for load in loads[1:]:
+        load.start()
 
     lo = pl.ds(0, half)
     hi = pl.ds(half, half)
     ring = {}
+    cross = []
 
     def ring_send(t, index, src, dst, target):
         copy = pltpu.make_async_remote_copy(
@@ -165,17 +168,36 @@
         ring[t, index] = copy
 
     def merge(t, q):
-        if t == 0:
-            loads[q].wait()
+        if t == (1 if q == 0 else 0):
+            if q:
+                loads[q].wait()
             pairs[q].wait_recv()
         for c in range(nbc):
             cols = pl.ds(c * block + t * LANES, LANES)
             acc[t, q, c] = loc[q, :, cols] + pair[q, :, cols]
 
-    def ring_one(t):
+    def ring_raw():
+        loads[0].wait()
+        other_in.wait()
+        for c in range(nbc):
+            cols = pl.ds(c * block, LANES)
+            acc[0, 0, c] = loc[0, :, cols]
+            raw[c] = other[:, cols]
+        ring_send(0, 0, acc.at[0, 0, lo], first_up.at[0], above)
+        ring_send(0, 1, acc.at[0, 0, hi], first_down.at[0], below)
+        for index, (part, target) in enumerate(((lo, above), (hi, below))):
+            copy = pltpu.make_async_remote_copy(
+                raw.at[part], crossed.at[index], cross_s.at[index], cross_r.at[index],
+                device_id=(target[0] + 1 - 2 * core, me_s), device_id_type=MESH)
+            copy.start()
+            cross.append(copy)
+
+    def ring_far(t):
         merge(t, 0)
         ring_send(t, 0, acc.at[t, 0, lo], first_up.at[t], above)
         ring_send(t, 1, acc.at[t, 0, hi], first_down.at[t], below)
+
+    def ring_one(t):
         merge(t, 1)
         ring_send(t, 2, acc.at[t, 1, hi], from_below.at[t, hi], above)
         merge(t, 2)
@@ -184,9 +206,15 @@
 
     def ring_two(t):
         ring[t, 0].wait_recv()
+        if t == 0:
+            cross[0].wait_recv()
+            first_up[0] = first_up[0] + crossed[0]
         acc[t, 1, lo] = acc[t, 1, lo] + first_up[t]
         ring_send(t, 4, acc.at[t, 1, lo], from_below.at[t, lo], above)
         ring[t, 1].wait_recv()
+        if t == 0:
+            cross[1].wait_recv()
+            first_down[0] = first_down[0] + crossed[1]
         acc[t, 2, hi] = acc[t, 2, hi] + first_down[t]
         ring_send(t, 5, acc.at[t, 2, hi], from_above.at[t, hi], below)
 
@@ -250,8 +278,16 @@
         ring_end(t)
         exchange_shards(t)
 
+    ring_raw()
+    for copy in pairs[1:]:
+        copy.start()
+    m_in.start()
+    v_in.start()
+    ring_far(1)
     ring_one(0)
     for t in range(1, chunks):
+        if t > 1:
+            ring_far(t)
         ring_one(t)
         if t == 1:
             for copy in lists:
@@ -296,7 +332,7 @@
     for copy in (m_out, v_out, a_out):
         copy.start()
 
-    for copy in pairs + list(ring.values()) + list(p1.values()):
+    for copy in pairs + cross + list(ring.values()) + list(p1.values()):
         copy.wait_send()
     for (t, k), copy in p2.items():
         if k < len(z_steps):
@@ -340,6 +376,9 @@
             pltpu.SMEM((1, LANES), jnp.int32),
             pltpu.VMEM((4, rows_dev, columns), f32),
             pltpu.VMEM((4, rows_dev, columns), f32),
+            pltpu.VMEM((rows_dev, columns), f32),
+            pltpu.VMEM((nbc,) + piece, f32),
+            pltpu.VMEM((2, nbc // 2) + piece, f32),
             pltpu.VMEM((chunks, 4, nbc) + piece, f32),
             pltpu.VMEM((chunks, nbc // 2) + piece, f32),
             pltpu.VMEM((chunks, nbc // 2) + piece, f32),
@@ -355,6 +394,8 @@
             dma((4,)),
             dma((4,)),
             dma((4,)),
+            dma((2,)),
+            dma((2,)),
             dma((chunks, 6)),
             dma((chunks, 6)),
             dma((chunks, nshard)),
@@ -362,7 +403,7 @@
             dma((chunks, ndp)),
             dma((chunks, ndp)),
             dma((3,)),
-            dma((2,)),
+            dma((3,)),
         ],
         compiler_params=pltpu.CompilerParams(
             collective_id=0, has_side_effects=True, vmem_limit_bytes=58 * MIB),

time: 87.2 us -> 86.6 us (level)
  no operation moved by 1% of the time
where the time goes in v4:
time: 86.6 us; the launch traced here: 86.4 us
  Pallas kernels  84.9 us (98%)
    pallas_call x1, Pallas kernels, forward(): pl.pallas_call(functools.partial(forward_kernel, dims, block), out_shape=...  43.5 us
    pallas_call x1, Pallas kernels, back(): pl.pallas_call(functools.partial(back_kernel, dims, block, rows_dev), out...  26.8 us
    pallas_call x1, Pallas kernels, owner_step(): pl.pallas_call(functools.partial(owner_kernel, step_place), out_shape=(sq...  14.5 us

profile of v4, /device:TPU:1, one launch (start us, length us, event | category | flops | bytes accessed | tf_op | source)
XLA Modules:
  0.0 86.4 jit_solution(12034611746985507122)
XLA Ops:
  0.6 43.5 %shard_map.126 = (f32[4,4,8,16,128]{4,3,2,1,0:T(8,128)}, f32[16,8192]{1,0:T(8,128)}, f32[16,8192]{1,0:T(8,128)}, f32[16,128]{1,0:T(8,128)}, s32[1,128]{1,0:T(1,128)}) custom-call(s32[1,64]{1,0:T(1,128)} %bitcast.23, s32[1,64]{1,0:T(1,128)} %bitcast.24, f32[128,8192]{1,0:T(8,128)} %bitcast.16, f32[16,8192]{1,0:T(8,128)} %bitcast.21, f32[16,8192]{1,0:T(8,128)} %bitcast.22), custom_call_target="tpu_custom_call" | custom-call | tf_op jit(solution)/shard_map/pallas_call | solution.py:362
  44.2 0.0 copy-start
  44.2 0.0 copy-start.1
  44.2 14.5 %shard_map.127 = (f32[512,512]{1,0:T(8,128)}, f32[512,512]{1,0:T(8,128)}, f32[512,512]{1,0:T(8,128)}, f32[512,512]{1,0:T(8,128)}, f32[16,8192]{1,0:T(8,128)}, /*index=5*/f32[16,8192]{1,0:T(8,128)}) custom-call(s32[1,128]{1,0:T(1,128)} %get-tuple-element.18.tab, f32[4,512,128]{2,1,0:T(8,128)} %bitcast.19, f32[512,512]{1,0:T(8,128)} %bitcast.25, ...), custom_call_target="tpu_custom_call" | custom-call | flops 13421772800 | bytes 9437184 | tf_op jit(solution)/shard_map/pallas_call | solution.py:544
  58.7 0.0 copy-done
  58.7 0.0 copy-done.1
  58.7 26.8 %shard_map.128 = f32[16,8192]{1,0:T(8,128)S(1)} custom-call(s32[1,128]{1,0:T(1,128)S(1)} %copy-done.1, f32[4,512,128]{2,1,0:T(8,128)} %bitcast.20, f32[512,512]{1,0:T(8,128)} %get-tuple-element.22.lroot, f32[512,512]{1,0:T(8,128)} %get-tuple-element.23.rroot, f32[16,128]{1,0:T(8,128)S(1)} %copy-done), custom_call_target="tpu_custom_call" | custom-call | tf_op jit(solution)/shard_map/pallas_call | solution.py:668
  85.6 0.8 copy.15
Async XLA Ops:
  44.2 14.5 %copy-start = (f32[16,128]{1,0:T(8,128)S(1)}, f32[16,128]{1,0:T(8,128)}, u32[]{:S(2)}) copy-start(f32[16,128]{1,0:T(8,128)} %get-tuple-element.24.adam) | copy-start | bytes 24580
  44.2 14.5 %copy-start.1 = (s32[1,128]{1,0:T(1,128)S(1)}, s32[1,128]{1,0:T(1,128)}, u32[]{:S(2)}) copy-start(s32[1,128]{1,0:T(1,128)} %get-tuple-element.18.tab) | copy-start | bytes 1540

commit v5 on v3

--- a/solution.py
+++ b/solution.py
@@ -102,11 +102,15 @@
     return (me_d // CORES + step[0]) % nz * CORES + (me_d % CORES + step[1]) % CORES
 
 
+def early_blocks(nbc):
+    return max(1, nbc // 8)
+
+
 def forward_kernel(dims, block, own, steps, grad, mom, sec,
                    gblk, mom_out, sec_out, adam_out, tab_out,
-                   ibuf, tvec, tab, loc, pair, acc, first_up, first_down, from_below, from_above,
+                   ibuf, tvec, tab, loc, pair, raw, acc, first_up, first_down, from_below, from_above,
                    gsel, mbuf, vbuf, send1, recv1, send2, asend,
-                   loc_sem, pair_s, pair_r, ring_s, ring_r, p1_s, p1_r, p2_s, p2_r,
+                   loc_sem, pair_s, pair_r, cross_s, cross_r, ring_s, ring_r, p1_s, p1_r, p2_s, p2_r,
                    io_sem, t_sem):
     ndp, nshard, nx, nbr, nbc = dims
     o_sends, o_rank, _, _, _ = offsets(dims)
@@ -133,11 +137,9 @@
     for q, step in enumerate(order):
         loads.append(pltpu.make_async_copy(
             grad.at[rows_of(zed(step), core), :], loc.at[q], loc_sem.at[q]))
-        loads[q].start()
+    loads[0].start()
     m_in = pltpu.make_async_copy(mom, mbuf, io_sem.at[0])
     v_in = pltpu.make_async_copy(sec, vbuf, io_sem.at[1])
-    m_in.start()
-    v_in.start()
 
     z_steps = dp_steps(ndp)
     s_steps = far_first(nshard, nx)
@@ -152,11 +154,15 @@
         pairs.append(pltpu.make_async_remote_copy(
             grad.at[rows_of(zed(step), 1 - core), :], pair.at[q],
             pair_s.at[q], pair_r.at[q], device_id=sibling, device_id_type=MESH))
-        pairs[q].start()
+    pairs[0].start()
 
     lo = pl.ds(0, half)
     hi = pl.ds(half, half)
+    early = early_blocks(nbc)
+    lo_rest = pl.ds(early, half - early)
+    hi_rest = pl.ds(half + early, half - early)
     ring = {}
+    cross = []
 
     def ring_send(t, index, src, dst, target):
         copy = pltpu.make_async_remote_copy(
@@ -172,10 +178,29 @@
             cols = pl.ds(c * block + t * LANES, LANES)
             acc[t, q, c] = loc[q, :, cols] + pair[q, :, cols]
 
+    def ring_raw():
+        for index in range(4):
+            side, swap = index // 2, index % 2
+            target = (above, below)[side]
+            copy = pltpu.make_async_remote_copy(
+                grad.at[rows_of(zed(order[0]), (core + swap) % CORES), pl.ds(side * half * block, early * block)],
+                raw.at[index], cross_s.at[index], cross_r.at[index],
+                device_id=(target[0] + swap * (1 - 2 * core), me_s), device_id_type=MESH)
+            copy.start()
+            cross.append(copy)
+
+    def ring_far(t):
+        merge(t, 0)
+        ring_send(t, 0, acc.at[t, 0, lo_rest], first_up.at[t], above)
+        ring_send(t, 1, acc.at[t, 0, hi_rest], first_down.at[t], below)
+
+    def add_raw(t, q, side):
+        for c in range(early):
+            cols = pl.ds(c * block + t * LANES, LANES)
+            acc[t, q, side * half + c] = acc[t, q, side * half + c] + (
+                raw[2 * side, :, cols] + raw[2 * side + 1, :, cols])
+
     def ring_one(t):
-        merge(t, 0)
-        ring_send(t, 0, acc.at[t, 0, lo], first_up.at[t], above)
-        ring_send(t, 1, acc.at[t, 0, hi], first_down.at[t], below)
         merge(t, 1)
         ring_send(t, 2, acc.at[t, 1, hi], from_below.at[t, hi], above)
         merge(t, 2)
@@ -184,10 +209,15 @@
 
     def ring_two(t):
         ring[t, 0].wait_recv()
-        acc[t, 1, lo] = acc[t, 1, lo] + first_up[t]
+        if t == 0:
+            for copy in cross:
+                copy.wait_recv()
+        add_raw(t, 1, 0)
+        acc[t, 1, lo_rest] = acc[t, 1, lo_rest] + first_up[t]
         ring_send(t, 4, acc.at[t, 1, lo], from_below.at[t, lo], above)
         ring[t, 1].wait_recv()
-        acc[t, 2, hi] = acc[t, 2, hi] + first_down[t]
+        add_raw(t, 2, 1)
+        acc[t, 2, hi_rest] = acc[t, 2, hi_rest] + first_down[t]
         ring_send(t, 5, acc.at[t, 2, hi], from_above.at[t, hi], below)
 
     def ring_end(t):
@@ -250,8 +280,18 @@
         ring_end(t)
         exchange_shards(t)
 
+    ring_raw()
+    for load, copy in zip(loads[1:], pairs[1:]):
+        load.start()
+        copy.start()
+    m_in.start()
+    v_in.start()
+    ring_far(0)
+    ring_far(1)
     ring_one(0)
     for t in range(1, chunks):
+        if t > 1:
+            ring_far(t)
         ring_one(t)
         if t == 1:
             for copy in lists:
@@ -296,7 +336,7 @@
     for copy in (m_out, v_out, a_out):
         copy.start()
 
-    for copy in pairs + list(ring.values()) + list(p1.values()):
+    for copy in pairs + cross + list(ring.values()) + list(p1.values()):
         copy.wait_send()
     for (t, k), copy in p2.items():
         if k < len(z_steps):
@@ -340,9 +380,10 @@
             pltpu.SMEM((1, LANES), jnp.int32),
             pltpu.VMEM((4, rows_dev, columns), f32),
             pltpu.VMEM((4, rows_dev, columns), f32),
+            pltpu.VMEM((4, rows_dev, early_blocks(nbc) * block), f32),
             pltpu.VMEM((chunks, 4, nbc) + piece, f32),
-            pltpu.VMEM((chunks, nbc // 2) + piece, f32),
-            pltpu.VMEM((chunks, nbc // 2) + piece, f32),
+            pltpu.VMEM((chunks, nbc // 2 - early_blocks(nbc)) + piece, f32),
+            pltpu.VMEM((chunks, nbc // 2 - early_blocks(nbc)) + piece, f32),
             pltpu.VMEM((chunks, nbc) + piece, f32),
             pltpu.VMEM((chunks, nbc) + piece, f32),
             pltpu.VMEM((chunks, nbc) + piece, f32),
@@ -352,6 +393,8 @@
             [pltpu.VMEM((nshard, CAP) + piece, f32) for _ in range(chunks)],
             pltpu.VMEM((chunks, ndp, nx) + piece, f32),
             pltpu.VMEM((nbc, LANES), f32),
+            dma((4,)),
+            dma((4,)),
             dma((4,)),
             dma((4,)),
             dma((4,)),
@@ -609,12 +652,9 @@
             p1[t, k].wait_recv()
         for c in range(nbc):
             cols = pl.ds(c * block + t * LANES, LANES)
-            out[:, cols] = recv1[t][tab[0, o_final + c]] * ad[c:c + 1, :]
-    done = pltpu.make_async_copy(out, update, io_sem.at[0])
-    done.start()
+            update[:, cols] = recv1[t][tab[0, o_final + c]] * ad[c:c + 1, :]
     for copy in list(p2.values()) + acopies + xcopies + list(p1.values()):
         copy.wait_send()
-    done.wait()
 
 
 def back(tab, gblk, lroot, rroot, adam, dims, block, rows_dev, columns):
@@ -628,7 +668,7 @@
         functools.partial(back_kernel, dims, block, rows_dev),
         out_shape=jax.ShapeDtypeStruct((rows_dev, columns), f32),
         in_specs=[pl.BlockSpec(memory_space=pltpu.SMEM)] + [hbm] * 4,
-        out_specs=pl.BlockSpec(memory_space=pl.ANY),
+        out_specs=pl.BlockSpec(memory_space=pltpu.VMEM),
         scratch_shapes=[
             pltpu.VMEM(gblk.shape, f32),
             pltpu.VMEM((block, block), f32),

time: 87.2 us -> 86.7 us (level)
    pallas_call x1, Pallas kernels: 44.4 us -> 43.3 us  [forward(): pl.pallas_call(functools.partial(forward_kernel, dims, block), out_shape=...]
where the time goes in v5:
time: 86.7 us; the launch traced here: 86.5 us
  Pallas kernels  85 us (98%)
    pallas_call x1, Pallas kernels, forward(): pl.pallas_call(functools.partial(forward_kernel, dims, block), out_shape=...  43.3 us
    pallas_call x1, Pallas kernels, back(): pl.pallas_call(functools.partial(back_kernel, dims, block, rows_dev), out...  27.2 us
    pallas_call x1, Pallas kernels, owner_step(): pl.pallas_call(functools.partial(owner_kernel, step_place), out_shape=(sq...  14.5 us

profile of v5, /device:TPU:1, one launch (start us, length us, event | category | flops | bytes accessed | tf_op | source)
XLA Modules:
  0.0 86.5 jit_solution(12557914877863997751)
XLA Ops:
  0.6 43.3 %shard_map.126 = (f32[4,4,8,16,128]{4,3,2,1,0:T(8,128)}, f32[16,8192]{1,0:T(8,128)}, f32[16,8192]{1,0:T(8,128)}, f32[16,128]{1,0:T(8,128)}, s32[1,128]{1,0:T(1,128)}) custom-call(s32[1,64]{1,0:T(1,128)} %bitcast.23, s32[1,64]{1,0:T(1,128)} %bitcast.24, f32[128,8192]{1,0:T(8,128)} %bitcast.16, f32[16,8192]{1,0:T(8,128)} %bitcast.21, f32[16,8192]{1,0:T(8,128)} %bitcast.22), custom_call_target="tpu_custom_call" | custom-call | tf_op jit(solution)/shard_map/pallas_call | solution.py:366
  44.0 0.0 copy-start
  44.0 0.0 copy-start.1
  44.0 14.5 %shard_map.127 = (f32[512,512]{1,0:T(8,128)}, f32[512,512]{1,0:T(8,128)}, f32[512,512]{1,0:T(8,128)}, f32[512,512]{1,0:T(8,128)}, f32[16,8192]{1,0:T(8,128)}, /*index=5*/f32[16,8192]{1,0:T(8,128)}) custom-call(s32[1,128]{1,0:T(1,128)} %get-tuple-element.18.tab, f32[4,512,128]{2,1,0:T(8,128)} %bitcast.19, f32[512,512]{1,0:T(8,128)} %bitcast.25, ...), custom_call_target="tpu_custom_call" | custom-call | flops 13421772800 | bytes 9437184 | tf_op jit(solution)/shard_map/pallas_call | solution.py:546
  58.5 0.0 copy-done
  58.5 0.0 copy-done.1
  58.5 27.2 %shard_map.128 = f32[16,8192]{1,0:T(8,128)S(1)} custom-call(s32[1,128]{1,0:T(1,128)S(1)} %copy-done.1, f32[4,512,128]{2,1,0:T(8,128)} %bitcast.20, f32[512,512]{1,0:T(8,128)} %get-tuple-element.22.lroot, f32[512,512]{1,0:T(8,128)} %get-tuple-element.23.rroot, f32[16,128]{1,0:T(8,128)S(1)} %copy-done), custom_call_target="tpu_custom_call" | custom-call | tf_op jit(solution)/shard_map/pallas_call | solution.py:667
  85.7 0.8 copy.15
Async XLA Ops:
  44.0 14.5 %copy-start = (f32[16,128]{1,0:T(8,128)S(1)}, f32[16,128]{1,0:T(8,128)}, u32[]{:S(2)}) copy-start(f32[16,128]{1,0:T(8,128)} %get-tuple-element.24.adam) | copy-start | bytes 24580
  44.0 14.5 %copy-start.1 = (s32[1,128]{1,0:T(1,128)S(1)}, s32[1,128]{1,0:T(1,128)}, u32[]{:S(2)}) copy-start(s32[1,128]{1,0:T(1,128)} %get-tuple-element.18.tab) | copy-start | bytes 1540
